TPU v7x, 32 devices: a whole 2x2x4 slice. The times are simulated.
32 devices in a mesh: path: 8 (over y, x, core), shard: 4 (over z).
Axes of the slice: x: 2, y: 2, z: 4, core: 2. Of those that a mesh axis runs over, the one named last changes fastest.
Arguments:
- path_delta: float32 [8, 2, 512, 1024], P('path', None, 'shard'), may hold values from -500 to 500
- assign: int32 [8, 2], replicated, may hold values from 0 to 15
- params: float32 [32, 4, 128, 1024], P(None, 'shard', 'path'), may hold values from -6 to 6
- momentum: float32 [32, 4, 128, 1024], P(None, 'shard', 'path'), may hold values from -3 to 3
Outputs:
- path_params: float32 [8, 2, 512, 1024], P('path', None, 'shard')
- new_params: float32 [32, 4, 128, 1024], P(None, 'shard', 'path')
- new_momentum: float32 [32, 4, 128, 1024], P(None, 'shard', 'path')
All inputs are finite; a program needn't handle non-finite values.
Results may differ from a plain program's by a relative error of at most 0.00007.
Values sent between devices are 32-bit elements; how exact they have to be, the bound alone decides.
No kernel may reach another device: no remote copies, remote signals or barrier semaphores. Data moves between devices by JAX's collectives and lax.ppermute only.
A program may use at most 128 MiB of HBM per device.

v0:
```python
import jax
import jax.numpy as jnp
from jax import lax
from jax.sharding import PartitionSpec as P

LEVEL_MODULES = 16
LEVELS = 2


outer_rate = 0.7
beta_coef = 0.9


def local(path_delta, assign, params, momentum):
    own_slab = path_delta[0]
    path_count = assign.shape[0]
    module_count = params.shape[0]
    own_rows = params.shape[2]
    width = own_slab.shape[2]
    squares = jnp.sum(own_slab * own_slab)
    total_sq = lax.psum(squares, "shard")
    entries = own_slab.shape[0] * own_slab.shape[1] * width * lax.axis_size("shard")
    rescale = 1.0 / jnp.sqrt(total_sq / entries + 1e-06)
    scaled = own_slab * rescale
    offsets = jnp.arange(LEVELS, dtype=jnp.int32) * LEVEL_MODULES
    module_id = assign + offsets[None, :]
    flat_ids = module_id.reshape(-1)
    membership = (flat_ids[:, None] == jnp.arange(module_count, dtype=jnp.int32)[None, :]).astype(
        jnp.float32
    )
    sharers = jnp.sum(membership, axis=0)
    path_here = lax.axis_index("path")
    own_members = lax.dynamic_slice_in_dim(membership, path_here * LEVELS, LEVELS, 0)
    summed = lax.psum_scatter(
        jnp.einsum("lm,lrd->rmd", own_members, scaled, precision=lax.Precision.HIGHEST),
        "path",
        scatter_dimension=0,
        tiled=True,
    )
    summed = jnp.transpose(summed, (1, 0, 2))
    outer_grad = summed / jnp.maximum(sharers, 1.0)[:, None, None]
    new_moment = beta_coef * momentum[:, 0] + outer_grad
    new_state = params[:, 0] - outer_rate * (outer_grad + beta_coef * new_moment)
    outgoing = jnp.take(new_state, flat_ids, axis=0).reshape(path_count, LEVELS, own_rows, width)
    returned = lax.all_to_all(outgoing, "path", split_axis=0, concat_axis=2, tiled=True)[0]
    return (returned[None], new_state[:, None], new_moment[:, None])


def solution(mesh):
    in_specs = (
        P("path", None, "shard", None),
        P(),
        P(None, "shard", "path", None),
        P(None, "shard", "path", None),
    )
    out_specs = (
        P("path", None, "shard", None),
        P(None, "shard", "path", None),
        P(None, "shard", "path", None),
    )
    return jax.shard_map(local, mesh=mesh, in_specs=in_specs, out_specs=out_specs, check_vma=False)
```

profile of v0, /device:TPU:0, one launch (start us, length us, event | category | flops | bytes accessed | tf_op | source)
XLA Modules:
  0.0 193.5 jit_solution(8089340344371571033)
XLA Ops:
  7.2 0.0 reduce-scatter.2.cloned.1.call-start
  7.2 0.8 compare_and_fusion
  8.0 0.1 copy.18
  8.1 0.1 reshape.61
  8.1 0.1 iota_compare_fusion
  8.2 2.1 %multiply_reduce_fusion = f32[]{:T(128)} fusion(f32[1,2,128,1024]{3,2,1,0:T(8,128)} %param.4), kind=kLoop, calls=%fused_computation.11 | loop fusion | flops 524287 | bytes 1048580 | tf_op jit(solution)/shard_map/reduce_sum | solution.py:20
  10.3 14.1 %psum.7 = f32[]{:T(128)} all-reduce(f32[]{:T(128)} %multiply_reduce_fusion), channel_id=1, replica_groups=mesh['path'=8,'shard'=4] {'shard'}, use_global_device_ids=true, to_apply=%region_1.0 | all-reduce | flops 1 | bytes 8 | tf_op jit(solution)/shard_map/psum | solution.py:21
  25.1 1.3 multiply_bitcast_fusion
  26.4 13.1 %convolution_bitcast_fusion = f32[128,32,1024]{2,1,0:T(8,128)} fusion(f32[2,128,1024]{2,1,0:T(8,128)S(1)} %multiply_bitcast_fusion, pred[16,32]{1,0:T(8,128)(4,1)S(1)} %iota_compare_fusion, s32[]{:T(128)S(6)} %select_n.26), kind=kOutput, calls=%fused_computation.1 | convolution fusion | flops 100663296 | bytes 17826308 | tf_op jit(solution)/shard_map/lm,lrd->rmd/dot_general | solution.py:35
  39.5 0.0 reduce-scatter.2.cloned.1.call-update
  39.5 0.1 reshape.62
  39.6 0.1 copy.16
  39.7 0.1 convert_reduce_fusion
  39.8 114.0 %reduce-scatter.2.cloned.1.call-done = f32[16,32,1024]{2,1,0:T(8,128)} async-done(((f32[128,32,1024]{2,1,0:T(8,128)}), f32[16,32,1024]{2,1,0:T(8,128)}) %reduce-scatter.2.cloned.1.call-update) | async-done | bytes 2097168 | tf_op jit(solution)/shard_map/reduce_scatter | solution.py:34
  153.8 7.1 %fusion.3 = (f32[32,1,16,1024]{3,0,2,1:T(8,128)}, f32[32,16,1024]{2,0,1:T(8,128)S(1)}) fusion(f32[32,1,16,1024]{3,2,1,0:T(8,128)} %param.7, f32[16,32,1024]{2,1,0:T(8,128)} %reduce-scatter.2.cloned.1.call-done, f32[32]{0:T(128)S(1)} %broadcast_maximum_fusion, f32[32,1,16,1024]{3,2,1,0:T(8,128)} %param.6), kind=kLoop, calls=%fused_computation.8 | loop fusion | flops 3670016 | bytes 10485888 | tf_op jit(solution)/shard_map/broadcast_in_dim | solution.py:46
  160.9 2.5 %copy.22 = f32[32,16,1024]{2,1,0:T(8,128)} copy(f32[32,16,1024]{2,0,1:T(8,128)S(1)} %get-tuple-element.12) | data formatting | bytes 4194304 | tf_op jit(solution)/shard_map/sub | solution.py:43
  163.4 2.2 %gather_fusion = f32[16,16,1024]{2,1,0:T(8,128)S(1)} fusion(f32[32,16,1024]{2,1,0:T(8,128)} %copy.22, s32[1024]{0:T(1024)S(1)} %pad_clamp_fusion), kind=kCustom, calls=%fused_computation | custom fusion | bytes 2097216 | tf_op jit(solution)/shard_map/jit(_take)/gather | solution.py:44
  165.6 1.1 broadcast_select_fusion
  166.7 3.6 %all-to-all-start = ((f32[8,2,16,1024]{3,2,1,0:T(8,128)}), f32[8,2,16,1024]{3,2,1,0:T(8,128)S(1)}, u32[]{:S(2)}, u32[]{:S(2)}) async-start(f32[8,2,16,1024]{3,2,1,0:T(8,128)} %broadcast_select_fusion), calls=%async_computation.1 | async-start | bytes 2097152 | tf_op jit(solution)/shard_map/all_to_all | solution.py:45
  170.3 0.0 copy-start
  170.3 2.5 %copy.24 = f32[32,1,16,1024]{3,2,1,0:T(8,128)} copy(f32[32,1,16,1024]{3,0,2,1:T(8,128)S(1)} %bitcast.36) | data formatting | bytes 4194304
  172.8 0.0 copy-done
  172.8 2.5 %copy.25 = f32[32,1,16,1024]{3,2,1,0:T(8,128)} copy(f32[32,1,16,1024]{3,0,2,1:T(8,128)S(1)} %copy-done) | data formatting | bytes 4194304
  175.4 10.3 %all-to-all-done = f32[8,2,16,1024]{3,2,1,0:T(8,128)S(1)} async-done(((f32[8,2,16,1024]{3,2,1,0:T(8,128)}), f32[8,2,16,1024]{3,2,1,0:T(8,128)S(1)}, u32[]{:S(2)}, u32[]{:S(2)}) %all-to-all-start) | async-done | bytes 1048608 | tf_op jit(solution)/shard_map/all_to_all | solution.py:45
  185.6 1.0 copy.23
  (4 shorter events, 0.0 us)
Async XLA Ops:
  7.2 146.6 %reduce-scatter.2.cloned.1.call-start = ((), (), s32[]{:S(2)}) async-start(), calls=%async_computation.2 | async-start | bytes 18874368 | tf_op jit(solution)/shard_map/reduce_scatter | solution.py:34
  166.7 18.9 %all-to-all-start = ((f32[8,2,16,1024]{3,2,1,0:T(8,128)}), f32[8,2,16,1024]{3,2,1,0:T(8,128)S(1)}, u32[]{:S(2)}, u32[]{:S(2)}) async-start(f32[8,2,16,1024]{3,2,1,0:T(8,128)} %broadcast_select_fusion), calls=%async_computation.1 | async-start | bytes 2097152 | tf_op jit(solution)/shard_map/all_to_all | solution.py:45
  170.3 2.6 %copy-start = (f32[32,1,16,1024]{3,0,2,1:T(8,128)S(1)}, f32[32,1,16,1024]{3,0,2,1:T(8,128)}, u32[]{:S(2)}) copy-start(f32[32,1,16,1024]{3,0,2,1:T(8,128)} %get-tuple-element.11) | copy-start | bytes 6291460
Sparse Core Ops, SparseCore 0:
  39.7 114.0 reduce-scatter.1
where the time goes:
time: 194 us
  waiting for transfers between devices  124 us (64%)
  between operations  14.8 us (8%)
  blocking collectives  14.1 us (7%)
  matrix products  13.1 us (7%)
  other arithmetic  12.5 us (6%)
  local copies, waits for them, and re-layouts  11.2 us (6%)
  starting transfers between devices  3.6 us (2%)
    reduce_scatter x1, waiting for transfers between devices, local(): lax.psum_scatter(jnp.einsum('lm,lrd->rmd', own_members, scaled, precision...  114 us
    psum x1, blocking collectives, local(): total_sq = lax.psum(squares, 'shard')  14.1 us
    dot_general x1, matrix products, local(): jnp.einsum('lm,lrd->rmd', own_members, scaled, precision=lax.Precision.HI...  13.1 us
    all_to_all x1, waiting for transfers between devices, local(): lax.all_to_all(outgoing, 'path', split_axis=0, concat_axis=2, tiled=True)[0]  10.3 us
    broadcast_in_dim x1, other arithmetic, local(): return (returned[None], new_state[:, None], new_moment[:, None])  7.07 us
    unnamed x4, local copies, waits for them, and re-layouts  5.08 us
  transfers between devices with their start and end apart: 2, of which 2 were waited for; matrix products, arithmetic and copies ran while one was open for 3% of the time, Pallas kernels for 0%

commit v1 on v0

v1 whole, which is shorter than its diff:
```python
import jax
import jax.numpy as jnp
from jax import lax
from jax.experimental import pallas as pl
from jax.experimental.pallas import tpu as pltpu
from jax.sharding import PartitionSpec as P

LEVEL_MODULES = 16
LEVELS = 2

outer_rate = 0.7
beta_coef = 0.9
moment_coef = outer_rate * beta_coef * beta_coef
grad_coef = outer_rate * (1.0 + beta_coef)

VMEM_LIMIT = 48 * 1024 * 1024


def params_of():
    return pltpu.CompilerParams(vmem_limit_bytes=VMEM_LIMIT)


def squares_kernel(delta_ref, out_ref):
    total = jnp.zeros(out_ref.shape, jnp.float32)
    for level in range(delta_ref.shape[0]):
        block = delta_ref[level]
        block = block * block
        folded = block.reshape(block.shape[0] // 8, 8, block.shape[1]).sum(axis=0)
        for lane in range(0, block.shape[1], 128):
            total = total + folded[:, lane : lane + 128]
    out_ref[...] = total


def gather_kernel(ids_ref, params_ref, momentum_ref, out_ref, param_rows, moment_rows, sems):
    path_count = out_ref.shape[1]
    copies = []
    for level in range(LEVELS):
        for path in range(path_count):
            module = ids_ref[path, level] + level * LEVEL_MODULES
            copies.append(
                (
                    pltpu.make_async_copy(params_ref.at[module], param_rows.at[level, path], sems.at[0, level, path]),
                    pltpu.make_async_copy(momentum_ref.at[module], moment_rows.at[level, path], sems.at[1, level, path]),
                )
            )
    for first, second in copies:
        first.start()
        second.start()
    for level in range(LEVELS):
        for path in range(path_count):
            first, second = copies[level * path_count + path]
            first.wait()
            second.wait()
            out_ref[level, path] = param_rows[level, path] - moment_coef * moment_rows[level, path]


def rescales(norm_ref, path_count, entries):
    shards = norm_ref.shape[0] // path_count
    result = []
    for path in range(path_count):
        tile = norm_ref[path * shards]
        for shard in range(1, shards):
            tile = tile + norm_ref[path * shards + shard]
        total = jnp.sum(tile, keepdims=True)
        result.append(1.0 / jnp.sqrt(total / entries + 1e-06))
    return result


def sharers_of(ids_ref, level, module):
    count = 0
    for path in range(ids_ref.shape[0]):
        count = count + (ids_ref[path, level] == module).astype(jnp.int32)
    return count


def outgoing_kernel(level, entries, ids_ref, norm_ref, received_ref, base_ref, out_ref):
    path_count = received_ref.shape[0]
    scale = rescales(norm_ref, path_count, entries)
    for path in range(path_count):
        module = ids_ref[path, level]
        weight = grad_coef / sharers_of(ids_ref, level, module).astype(jnp.float32)
        total = base_ref[path]
        for other in range(path_count):
            factor = jnp.where(ids_ref[other, level] == module, weight, 0.0)
            total = total - (scale[other] * factor) * received_ref[other]
        out_ref[path] = total


def state_kernel(level, entries, ids_ref, norm_ref, received_ref, params_ref, momentum_ref, *outs):
    new_params_ref, new_momentum_ref = outs[-2:]
    path_count = received_ref.shape[0]
    scale = rescales(norm_ref, path_count, entries)
    count = params_ref.shape[0]
    for place in range(count):
        module = pl.program_id(0) * count + place
        sharers = jnp.maximum(sharers_of(ids_ref, level, module), 1)
        weight = 1.0 / sharers.astype(jnp.float32)
        grad = jnp.zeros(received_ref.shape[1:], jnp.float32)
        for other in range(path_count):
            factor = jnp.where(ids_ref[other, level] == module, weight, 0.0)
            grad = grad + (scale[other] * factor) * received_ref[other]
        new_moment = beta_coef * momentum_ref[place] + grad
        new_momentum_ref[place] = new_moment
        new_params_ref[place] = params_ref[place] - outer_rate * (grad + beta_coef * new_moment)


def local(path_delta, assign, params, momentum):
    own_slab = path_delta[0]
    path_count = assign.shape[0]
    module_count = params.shape[0]
    own_rows = params.shape[2]
    width = own_slab.shape[2]
    shards = lax.axis_size("shard")
    entries = float(own_slab.shape[0] * own_slab.shape[1] * width * shards)
    state_in = params.reshape(module_count, own_rows, width)
    moment_in = momentum.reshape(module_count, own_rows, width)
    vmem = pl.BlockSpec(memory_space=pltpu.VMEM)
    smem = pl.BlockSpec(memory_space=pltpu.SMEM)
    anywhere = pl.BlockSpec(memory_space=pl.ANY)

    squares = pl.pallas_call(
        squares_kernel,
        out_shape=jax.ShapeDtypeStruct((8, 128), jnp.float32),
        in_specs=[vmem],
        out_specs=vmem,
        compiler_params=params_of(),
    )(own_slab)
    norms = lax.all_to_all(
        jnp.broadcast_to(squares[None], (path_count * shards, 8, 128)),
        ("path", "shard"),
        split_axis=0,
        concat_axis=0,
        tiled=True,
    )
    received = [
        lax.all_to_all(
            own_slab[level].reshape(path_count, own_rows, width), "path", split_axis=0, concat_axis=0, tiled=True
        )
        for level in range(LEVELS)
    ]
    base = pl.pallas_call(
        gather_kernel,
        out_shape=jax.ShapeDtypeStruct((LEVELS, path_count, own_rows, width), jnp.float32),
        in_specs=[smem, anywhere, anywhere],
        out_specs=vmem,
        scratch_shapes=[
            pltpu.VMEM((LEVELS, path_count, own_rows, width), jnp.float32),
            pltpu.VMEM((LEVELS, path_count, own_rows, width), jnp.float32),
            pltpu.SemaphoreType.DMA((2, LEVELS, path_count)),
        ],
        compiler_params=params_of(),
    )(assign, state_in, moment_in)
    returned = []
    for level in range(LEVELS):
        outgoing = pl.pallas_call(
            lambda *refs, level=level: outgoing_kernel(level, entries, *refs),
            out_shape=jax.ShapeDtypeStruct((path_count, own_rows, width), jnp.float32),
            in_specs=[smem, vmem, vmem, vmem],
            out_specs=vmem,
            compiler_params=params_of(),
        )(assign, norms, received[level], base[level])
        returned.append(
            lax.all_to_all(outgoing, "path", split_axis=0, concat_axis=0, tiled=True).reshape(
                path_count * own_rows, width
            )
        )
    new_state, new_moment = None, None
    block = 4
    steps = LEVEL_MODULES // block
    for level in range(LEVELS):
        level_block = pl.BlockSpec((block, own_rows, width), lambda i, level=level: (i + level * steps, 0, 0))
        call_in = [assign, norms, received[level], state_in, moment_in]
        in_specs = [smem, vmem, vmem, level_block, level_block]
        kernel = lambda *refs, level=level: state_kernel(level, entries, *refs)
        aliases = {}
        if level:
            call_in += [new_state, new_moment]
            in_specs += [anywhere, anywhere]
            aliases = {5: 0, 6: 1}
        new_state, new_moment = pl.pallas_call(
            kernel,
            grid=(steps,),
            out_shape=[jax.ShapeDtypeStruct(state_in.shape, jnp.float32)] * 2,
            in_specs=in_specs,
            out_specs=[level_block, level_block],
            input_output_aliases=aliases,
            compiler_params=params_of(),
        )(*call_in)
    return (jnp.stack(returned)[None], new_state[:, None], new_moment[:, None])


def solution(mesh):
    in_specs = (
        P("path", None, "shard", None),
        P(),
        P(None, "shard", "path", None),
        P(None, "shard", "path", None),
    )
    out_specs = (
        P("path", None, "shard", None),
        P(None, "shard", "path", None),
        P(None, "shard", "path", None),
    )
    return jax.shard_map(local, mesh=mesh, in_specs=in_specs, out_specs=out_specs, check_vma=False)
```

time: 194 us -> 75.4 us (0.39)
  waiting for transfers between devices: 124 us -> 17.3 us
  starting transfers between devices: 3.6 us -> 19.1 us
  between operations: 14.8 us -> 0.77 us
  matrix products: 13.1 us -> 0 us
  Pallas kernels: 0 us -> 12.4 us
  other arithmetic: 12.5 us -> 2.28 us
    reduce_scatter x1 -> x0, waiting for transfers between devices: 114 us -> none  [local(): lax.psum_scatter(jnp.einsum('lm,lrd->rmd', own_members, scaled, precision...]
    all_to_all x1 -> x4, starting transfers between devices: 3.56 us -> 19.1 us  [the longest x2 8.29 us: local(): lax.all_to_all(outgoing, 'path', split_axis=0, concat_axis=0, tiled=True)]
    psum x1 -> x0, blocking collectives: 14.1 us -> none  [local(): total_sq = lax.psum(squares, 'shard')]
    all_to_all x0 -> x1, blocking collectives: none -> 13.1 us  [local(): lax.all_to_all(own_slab[level].reshape(path_count, own_rows, width), 'pat...]
    dot_general x1 -> x0, matrix products: 13.1 us -> none  [local(): jnp.einsum('lm,lrd->rmd', own_members, scaled, precision=lax.Precision.HI...]
    pallas_call x0 -> x6, Pallas kernels: none -> 12.4 us  [the longest x2 6.43 us: local(): pl.pallas_call(kernel, grid=(steps,), out_shape=[jax.ShapeDtypeStruct(sta...]
    all_to_all x1 -> x4, waiting for transfers between devices: 10.3 us -> 17.3 us  [the longest x2 8.59 us: local(): lax.all_to_all(outgoing, 'path', split_axis=0, concat_axis=0, tiled=True)]
    broadcast_in_dim x1, other arithmetic: 7.07 us -> 2.28 us  [local(): return (jnp.stack(returned)[None], new_state[:, None], new_moment[:, None])]
  transfers between devices with their start and end apart: 2 -> 4, of which waited for: 2 -> 4; matrix products, arithmetic and copies ran while one was open for 3% -> 3% of each run, Pallas kernels for 0% -> 16%
where the time goes in v1:
time: 75.4 us; the launch traced here: 74.7 us
  starting transfers between devices  19.1 us (25%)
  waiting for transfers between devices  17.3 us (23%)
  blocking collectives  13.1 us (17%)
  Pallas kernels  12.4 us (16%)
  local copies, waits for them, and re-layouts  9.72 us (13%)
  other arithmetic  2.28 us (3%)
  between operations  0.77 us (1%)
    all_to_all x1, blocking collectives, local(): lax.all_to_all(own_slab[level].reshape(path_count, own_rows, width), 'pat...  13.1 us
    all_to_all x2, waiting for transfers between devices, local(): lax.all_to_all(outgoing, 'path', split_axis=0, concat_axis=0, tiled=True)  8.59 us
    all_to_all x2, starting transfers between devices, local(): lax.all_to_all(outgoing, 'path', split_axis=0, concat_axis=0, tiled=True)  8.29 us
    all_to_all x1, waiting for transfers between devices, local(): lax.all_to_all(jnp.broadcast_to(squares[None], (path_count * shards, 8, 1...  7.33 us
    all_to_all x1, starting transfers between devices, local(): lax.all_to_all(jnp.broadcast_to(squares[None], (path_count * shards, 8, 1...  7.3 us
    unnamed x19, local copies, waits for them, and re-layouts  7.11 us
    pallas_call x2, Pallas kernels, local(): pl.pallas_call(kernel, grid=(steps,), out_shape=[jax.ShapeDtypeStruct(sta...  6.43 us
    pallas_call x1, Pallas kernels, local(): pl.pallas_call(gather_kernel, out_shape=jax.ShapeDtypeStruct((LEVELS, pat...  3.82 us
  transfers between devices with their start and end apart: 4, of which 4 were waited for; matrix products, arithmetic and copies ran while one was open for 3% of the time, Pallas kernels for 16%

profile of v1, /device:TPU:0, one launch (start us, length us, event | category | flops | bytes accessed | tf_op | source)
XLA Modules:
  0.0 74.7 jit_solution(1691040853092536048)
XLA Ops:
  0.6 0.0 copy-start.3
  0.6 1.2 %copy-done.3 = f32[1,2,128,1024]{3,2,1,0:T(8,128)S(1)} copy-done((f32[1,2,128,1024]{3,2,1,0:T(8,128)S(1)}, f32[1,2,128,1024]{3,2,1,0:T(8,128)}, u32[]{:S(2)}) %copy-start.3) | copy-done | bytes 1048600
  1.9 0.0 copy-start.4
  1.9 0.1 shard_map.67
  1.9 0.7 broadcast_in_dim.15
  2.6 7.3 %all-to-all-start = ((f32[32,8,128]{2,1,0:T(8,128)}), f32[32,8,128]{2,1,0:T(8,128)S(1)}, u32[]{:S(2)}, u32[]{:S(2)}) async-start(f32[32,8,128]{2,1,0:T(8,128)} %broadcast_in_dim.15), calls=%async_computation | async-start | bytes 262144 | tf_op jit(solution)/shard_map/all_to_all | solution.py:128
  9.9 0.0 copy-done.4
  9.9 0.0 copy-start.8
  9.9 0.0 copy-start
  10.0 1.0 %fusion = (f32[1,1,128,1024]{3,2,1,0:T(8,128)}, f32[1,1,128,1024]{3,2,1,0:T(8,128)}) fusion(f32[1,2,128,1024]{3,2,1,0:T(8,128)S(1)} %copy-done.4), kind=kLoop, calls=%fused_computation.3 | loop fusion | bytes 2097152 | tf_op jit(solution)/shard_map/slice | solution.py:137
  11.0 7.3 %all-to-all-done.refs_1_ = f32[32,8,128]{2,1,0:T(8,128)S(1)} async-done(((f32[32,8,128]{2,1,0:T(8,128)}), f32[32,8,128]{2,1,0:T(8,128)S(1)}, u32[]{:S(2)}, u32[]{:S(2)}) %all-to-all-start) | async-done | bytes 131104 | tf_op jit(solution)/shard_map/all_to_all | solution.py:128
  18.3 13.1 %all_to_all.25.refs_2_ = f32[8,16,1024]{2,1,0:T(8,128)S(1)} all-to-all(f32[8,16,1024]{2,1,0:T(8,128)} %bitcast.27), channel_id=1, replica_groups=mesh['path'=8,'shard'=4] {'path'}, dimensions={0} | all-to-all | bytes 1048576 | tf_op jit(solution)/shard_map/all_to_all | solution.py:136
  31.5 3.5 %all-to-all-start.3 = ((f32[8,16,1024]{2,1,0:T(8,128)}), f32[8,16,1024]{2,1,0:T(8,128)S(1)}, u32[]{:S(2)}, u32[]{:S(2)}) async-start(f32[8,16,1024]{2,1,0:T(8,128)} %bitcast.26), calls=%async_computation.3 | async-start | bytes 1048576 | tf_op jit(solution)/shard_map/all_to_all | solution.py:136
  35.0 0.0 copy-done.8
  35.0 0.1 copy.10.ids_ref.refs_0_
  35.1 0.0 copy-done
  35.1 0.0 copy-start.1
  35.1 1.6 %copy-done.1 = f32[32,1,16,1024]{3,2,1,0:T(8,128)S(1)} copy-done((f32[32,1,16,1024]{3,2,1,0:T(8,128)S(1)}, f32[32,1,16,1024]{3,2,1,0:T(8,128)}, u32[]{:S(2)}) %copy-start.1) | copy-done | bytes 2097176
  36.7 3.8 %shard_map.68 = f32[2,8,16,1024]{3,2,1,0:T(8,128)S(1)} custom-call(s32[8,2]{1,0:T(8,128)S(1)} %copy.10.ids_ref.refs_0_, f32[32,16,1024]{2,1,0:T(8,128)S(1)} %bitcast.19, f32[32,16,1024]{2,1,0:T(8,128)S(1)} %bitcast.22), custom_call_target="tpu_custom_call" | custom-call | tf_op jit(solution)/shard_map/pallas_call | solution.py:141
  40.5 0.9 %slice_bitcast_fusion.1 = (f32[8,16,1024]{2,1,0:T(8,128)S(1)}, f32[8,16,1024]{2,1,0:T(8,128)}) fusion(f32[2,8,16,1024]{3,2,1,0:T(8,128)S(1)} %shard_map.68), kind=kLoop, calls=%fused_computation.2 | loop fusion | bytes 2097152 | tf_op jit(solution)/shard_map/squeeze | solution.py:161
  41.4 1.0 %shard_map.69 = f32[8,16,1024]{2,1,0:T(8,128)S(1)} custom-call(s32[8,2]{1,0:T(8,128)S(1)} %copy.10.ids_ref.refs_0_, f32[32,8,128]{2,1,0:T(8,128)S(1)} %all-to-all-done.refs_1_, f32[8,16,1024]{2,1,0:T(8,128)S(1)} %all_to_all.25.refs_2_, f32[8,16,1024]{2,1,0:T(8,128)S(1)} %get-tuple-element.14.refs_3_), custom_call_target="tpu_custom_call" | custom-call | tf_op jit(solution)/shard_map/pallas_call | solution.py:155
  42.4 0.0 copy-start.6
  42.5 0.8 %copy-done.6 = f32[8,16,1024]{2,1,0:T(8,128)} copy-done((f32[8,16,1024]{2,1,0:T(8,128)}, f32[8,16,1024]{2,1,0:T(8,128)S(1)}, u32[]{:S(2)}) %copy-start.6) | copy-done | bytes 524312
  43.2 1.4 %all-to-all-done.3.refs_2_ = f32[8,16,1024]{2,1,0:T(8,128)S(1)} async-done(((f32[8,16,1024]{2,1,0:T(8,128)}), f32[8,16,1024]{2,1,0:T(8,128)S(1)}, u32[]{:S(2)}, u32[]{:S(2)}) %all-to-all-start.3) | async-done | bytes 524320 | tf_op jit(solution)/shard_map/all_to_all | solution.py:136
  44.6 4.1 %all-to-all-start.2 = ((f32[8,16,1024]{2,1,0:T(8,128)}), f32[8,16,1024]{2,1,0:T(8,128)}, u32[]{:S(2)}, u32[]{:S(2)}) async-start(f32[8,16,1024]{2,1,0:T(8,128)} %copy-done.6), calls=%async_computation.2 | async-start | bytes 1048576 | tf_op jit(solution)/shard_map/all_to_all | solution.py:163
  48.8 0.0 copy-start.7
  48.8 1.0 %copy-done.7 = f32[8,16,1024]{2,1,0:T(8,128)S(1)} copy-done((f32[8,16,1024]{2,1,0:T(8,128)S(1)}, f32[8,16,1024]{2,1,0:T(8,128)}, u32[]{:S(2)}) %copy-start.7) | copy-done | bytes 524312
  49.8 1.0 %shard_map.70 = f32[8,16,1024]{2,1,0:T(8,128)S(1)} custom-call(s32[8,2]{1,0:T(8,128)S(1)} %copy.10.ids_ref.refs_0_, f32[32,8,128]{2,1,0:T(8,128)S(1)} %all-to-all-done.refs_1_, f32[8,16,1024]{2,1,0:T(8,128)S(1)} %all-to-all-done.3.refs_2_, f32[8,16,1024]{2,1,0:T(8,128)S(1)} %copy-done.7), custom_call_target="tpu_custom_call" | custom-call | tf_op jit(solution)/shard_map/pallas_call | solution.py:155
  50.9 0.0 copy-start.5
  50.9 0.8 %copy-done.5 = f32[8,16,1024]{2,1,0:T(8,128)} copy-done((f32[8,16,1024]{2,1,0:T(8,128)}, f32[8,16,1024]{2,1,0:T(8,128)S(1)}, u32[]{:S(2)}) %copy-start.5) | copy-done | bytes 524312
  51.7 6.9 %all-to-all-done.2 = f32[8,16,1024]{2,1,0:T(8,128)} async-done(((f32[8,16,1024]{2,1,0:T(8,128)}), f32[8,16,1024]{2,1,0:T(8,128)}, u32[]{:S(2)}, u32[]{:S(2)}) %all-to-all-start.2) | async-done | bytes 524320 | tf_op jit(solution)/shard_map/all_to_all | solution.py:163
  58.5 4.2 %all-to-all-start.4 = ((f32[8,16,1024]{2,1,0:T(8,128)}), f32[8,16,1024]{2,1,0:T(8,128)}, u32[]{:S(2)}, u32[]{:S(2)}) async-start(f32[8,16,1024]{2,1,0:T(8,128)} %copy-done.5), calls=%async_computation.4 | async-start | bytes 1048576 | tf_op jit(solution)/shard_map/all_to_all | solution.py:163
  62.7 0.0 copy-start.2
  62.7 1.6 %copy-done.2 = f32[32,1,16,1024]{3,2,1,0:T(8,128)S(1)} copy-done((f32[32,1,16,1024]{3,2,1,0:T(8,128)S(1)}, f32[32,1,16,1024]{3,2,1,0:T(8,128)}, u32[]{:S(2)}) %copy-start.2) | copy-done | bytes 2097176
  64.3 3.2 %shard_map.71 = (f32[32,16,1024]{2,1,0:T(8,128)}, f32[32,16,1024]{2,1,0:T(8,128)}) custom-call(s32[8,2]{1,0:T(8,128)S(1)} %copy.10.ids_ref.refs_0_, f32[32,8,128]{2,1,0:T(8,128)S(1)} %all-to-all-done.refs_1_, f32[8,16,1024]{2,1,0:T(8,128)S(1)} %all_to_all.25.refs_2_, f32[32,16,1024]{2,1,0:T(8,128)S(1)} %bitcast.20, f32[32,16,1024]{2,1,0:T(8,128)S(1)} %bitcast.23), custom_call_target="tpu_custom_call" | custom-call | tf_op jit(solution)/shard_map/pallas_call | solution.py:180
  67.5 3.2 %shard_map.72 = (f32[32,16,1024]{2,1,0:T(8,128)}, f32[32,16,1024]{2,1,0:T(8,128)}) custom-call(s32[8,2]{1,0:T(8,128)S(1)} %copy.10.ids_ref.refs_0_, f32[32,8,128]{2,1,0:T(8,128)S(1)} %all-to-all-done.refs_1_, f32[8,16,1024]{2,1,0:T(8,128)S(1)} %all-to-all-done.3.refs_2_, f32[32,16,1024]{2,1,0:T(8,128)S(1)} %bitcast.21, ...), custom_call_target="tpu_custom_call", output_to_operand_aliasing={{0}: (5, {}), {1}: (6, {})} | custom-call | tf_op jit(solution)/shard_map/pallas_call | solution.py:180
  70.7 1.7 %all-to-all-done.4 = f32[8,16,1024]{2,1,0:T(8,128)} async-done(((f32[8,16,1024]{2,1,0:T(8,128)}), f32[8,16,1024]{2,1,0:T(8,128)}, u32[]{:S(2)}, u32[]{:S(2)}) %all-to-all-start.4) | async-done | bytes 524320 | tf_op jit(solution)/shard_map/all_to_all | solution.py:163
  72.5 2.3 %maximum_bitcast_fusion = f32[1,2,128,1024]{3,2,1,0:T(8,128)} fusion(f32[1,128,1024]{2,1,0:T(8,128)} %bitcast.8, f32[1,128,1024]{2,1,0:T(8,128)} %bitcast.5), kind=kLoop, calls=%fused_computation | loop fusion | flops 262144 | bytes 2097152 | tf_op jit(solution)/shard_map/broadcast_in_dim | solution.py:189
Async XLA Ops:
  0.6 1.2 %copy-start.3 = (f32[1,2,128,1024]{3,2,1,0:T(8,128)S(1)}, f32[1,2,128,1024]{3,2,1,0:T(8,128)}, u32[]{:S(2)}) copy-start(f32[1,2,128,1024]{3,2,1,0:T(8,128)} %param.4) | copy-start | bytes 3145732
  1.9 8.1 %copy-start.4 = (f32[1,2,128,1024]{3,2,1,0:T(8,128)S(1)}, f32[1,2,128,1024]{3,2,1,0:T(8,128)}, u32[]{:S(2)}) copy-start(f32[1,2,128,1024]{3,2,1,0:T(8,128)} %param.4) | copy-start | bytes 3145732
  2.6 15.7 %all-to-all-start = ((f32[32,8,128]{2,1,0:T(8,128)}), f32[32,8,128]{2,1,0:T(8,128)S(1)}, u32[]{:S(2)}, u32[]{:S(2)}) async-start(f32[32,8,128]{2,1,0:T(8,128)} %broadcast_in_dim.15), calls=%async_computation | async-start | bytes 262144 | tf_op jit(solution)/shard_map/all_to_all | solution.py:128
  9.9 25.0 %copy-start.8 = (s32[8,2]{0,1:T(2,128)S(1)}, s32[8,2]{0,1:T(2,128)}, u32[]{:S(2)}) copy-start(s32[8,2]{0,1:T(2,128)} %param.5) | copy-start | bytes 196
  9.9 25.1 %copy-start = (f32[32,1,16,1024]{3,2,1,0:T(8,128)S(1)}, f32[32,1,16,1024]{3,2,1,0:T(8,128)}, u32[]{:S(2)}) copy-start(f32[32,1,16,1024]{3,2,1,0:T(8,128)} %param.6) | copy-start | bytes 6291460
  31.5 13.2 %all-to-all-start.3 = ((f32[8,16,1024]{2,1,0:T(8,128)}), f32[8,16,1024]{2,1,0:T(8,128)S(1)}, u32[]{:S(2)}, u32[]{:S(2)}) async-start(f32[8,16,1024]{2,1,0:T(8,128)} %bitcast.26), calls=%async_computation.3 | async-start | bytes 1048576 | tf_op jit(solution)/shard_map/all_to_all | solution.py:136
  35.1 1.6 %copy-start.1 = (f32[32,1,16,1024]{3,2,1,0:T(8,128)S(1)}, f32[32,1,16,1024]{3,2,1,0:T(8,128)}, u32[]{:S(2)}) copy-start(f32[32,1,16,1024]{3,2,1,0:T(8,128)} %param.7) | copy-start | bytes 6291460
  42.4 0.8 %copy-start.6 = (f32[8,16,1024]{2,1,0:T(8,128)}, f32[8,16,1024]{2,1,0:T(8,128)S(1)}, u32[]{:S(2)}) copy-start(f32[8,16,1024]{2,1,0:T(8,128)S(1)} %shard_map.69) | copy-start | bytes 1572868
  44.6 13.9 %all-to-all-start.2 = ((f32[8,16,1024]{2,1,0:T(8,128)}), f32[8,16,1024]{2,1,0:T(8,128)}, u32[]{:S(2)}, u32[]{:S(2)}) async-start(f32[8,16,1024]{2,1,0:T(8,128)} %copy-done.6), calls=%async_computation.2 | async-start | bytes 1048576 | tf_op jit(solution)/shard_map/all_to_all | solution.py:163
  48.8 1.0 %copy-start.7 = (f32[8,16,1024]{2,1,0:T(8,128)S(1)}, f32[8,16,1024]{2,1,0:T(8,128)}, u32[]{:S(2)}) copy-start(f32[8,16,1024]{2,1,0:T(8,128)} %get-tuple-element.15.refs_3_) | copy-start | bytes 1572868
  50.9 0.8 %copy-start.5 = (f32[8,16,1024]{2,1,0:T(8,128)}, f32[8,16,1024]{2,1,0:T(8,128)S(1)}, u32[]{:S(2)}) copy-start(f32[8,16,1024]{2,1,0:T(8,128)S(1)} %shard_map.70) | copy-start | bytes 1572868
  58.5 13.9 %all-to-all-start.4 = ((f32[8,16,1024]{2,1,0:T(8,128)}), f32[8,16,1024]{2,1,0:T(8,128)}, u32[]{:S(2)}, u32[]{:S(2)}) async-start(f32[8,16,1024]{2,1,0:T(8,128)} %copy-done.5), calls=%async_computation.4 | async-start | bytes 1048576 | tf_op jit(solution)/shard_map/all_to_all | solution.py:163
  62.7 1.6 %copy-start.2 = (f32[32,1,16,1024]{3,2,1,0:T(8,128)S(1)}, f32[32,1,16,1024]{3,2,1,0:T(8,128)}, u32[]{:S(2)}) copy-start(f32[32,1,16,1024]{3,2,1,0:T(8,128)} %param.7) | copy-start | bytes 6291460

commit v2 on v0

v2 whole, which is shorter than its diff:
```python
import jax
import jax.numpy as jnp
from jax import lax
from jax.experimental import pallas as pl
from jax.experimental.pallas import tpu as pltpu
from jax.sharding import PartitionSpec as P

LEVEL_MODULES = 16
LEVELS = 2

outer_rate = 0.7
beta_coef = 0.9
moment_coef = outer_rate * beta_coef * beta_coef
grad_coef = outer_rate * (1.0 + beta_coef)

VMEM_LIMIT = 48 * 1024 * 1024

vmem = pl.BlockSpec(memory_space=pltpu.VMEM)
smem = pl.BlockSpec(memory_space=pltpu.SMEM)
anywhere = pl.BlockSpec(memory_space=pl.ANY)


def call(kernel, out_shape, in_specs, out_specs, **more):
    return pl.pallas_call(
        kernel,
        out_shape=out_shape,
        in_specs=in_specs,
        out_specs=out_specs,
        compiler_params=pltpu.CompilerParams(vmem_limit_bytes=VMEM_LIMIT),
        **more,
    )


def exchange(arrays, axis):
    size = lax.axis_size(axis)
    return [arrays[0]] + [
        lax.ppermute(arrays[k], axis, [(i, i ^ k) for i in range(size)]) for k in range(1, size)
    ]


def squares_kernel(delta_ref, out_ref):
    total = jnp.zeros(out_ref.shape, jnp.float32)
    for level in range(delta_ref.shape[0]):
        block = delta_ref[level]
        block = block * block
        folded = block.reshape(block.shape[0] // 8, 8, block.shape[1]).sum(axis=0)
        for lane in range(0, block.shape[1], 128):
            total = total + folded[:, lane : lane + 128]
    out_ref[...] = total


def pack_kernel(entries, shards, here_ref, delta_ref, *refs):
    tiles, outs = refs[:shards], refs[shards:]
    tile = tiles[0][...]
    for other in tiles[1:]:
        tile = tile + other[...]
    rescale = 1.0 / jnp.sqrt(jnp.sum(tile, keepdims=True) / entries + 1e-06)
    for k, out in enumerate(outs):
        for level in range(LEVELS):
            out[level] = delta_ref[level, here_ref[0] ^ k] * rescale


def gather_kernel(here_ref, ids_ref, params_ref, momentum_ref, out_ref, param_rows, moment_rows, sems):
    path_count = out_ref.shape[1]
    copies = []
    for level in range(LEVELS):
        for k in range(path_count):
            module = ids_ref[here_ref[0] ^ k, level] + level * LEVEL_MODULES
            copies.append(
                (
                    pltpu.make_async_copy(params_ref.at[module], param_rows.at[level, k], sems.at[0, level, k]),
                    pltpu.make_async_copy(momentum_ref.at[module], moment_rows.at[level, k], sems.at[1, level, k]),
                )
            )
    for first, second in copies:
        first.start()
        second.start()
    for level in range(LEVELS):
        for k in range(path_count):
            first, second = copies[level * path_count + k]
            first.wait()
            second.wait()
            out_ref[level, k] = param_rows[level, k] - moment_coef * moment_rows[level, k]


def sharers_of(ids_ref, level, module):
    count = 0
    for path in range(ids_ref.shape[0]):
        count = count + (ids_ref[path, level] == module).astype(jnp.int32)
    return jnp.maximum(count, 1).astype(jnp.float32)


def outgoing_kernel(path_count, here_ref, ids_ref, base_ref, *refs):
    received, outs = refs[:path_count], refs[path_count:]
    here = here_ref[0]
    for level in range(LEVELS):
        for k in range(path_count):
            module = ids_ref[here ^ k, level]
            weight = grad_coef / sharers_of(ids_ref, level, module)
            total = base_ref[level, k]
            for other in range(path_count):
                factor = jnp.where(ids_ref[here ^ other, level] == module, weight, 0.0)
                total = total - factor * received[other][level]
            outs[k][level] = total


def state_kernel(path_count, here_ref, ids_ref, *refs):
    received = refs[:path_count]
    params_ref, momentum_ref, new_params_ref, new_momentum_ref = refs[path_count:]
    here = here_ref[0]
    count = params_ref.shape[0]
    first = pl.program_id(0) * count
    level = first // LEVEL_MODULES
    for place in range(count):
        module = first + place - level * LEVEL_MODULES
        weight = 1.0 / sharers_of(ids_ref, level, module)
        grad = jnp.zeros(params_ref.shape[1:], jnp.float32)
        for other in range(path_count):
            factor = jnp.where(ids_ref[here ^ other, level] == module, weight, 0.0)
            grad = grad + factor * received[other][level]
        new_moment = beta_coef * momentum_ref[place] + grad
        new_momentum_ref[place] = new_moment
        new_params_ref[place] = params_ref[place] - outer_rate * (grad + beta_coef * new_moment)


def assemble_kernel(path_count, here_ref, *refs):
    returned, out_ref, sems = refs[:path_count], refs[path_count], refs[path_count + 1]
    copies = []
    for k in range(path_count):
        copies.append(pltpu.make_async_copy(returned[k], out_ref.at[:, here_ref[0] ^ k], sems.at[k]))
    for copy in copies:
        copy.start()
    for copy in copies:
        copy.wait()


def local(path_delta, assign, params, momentum):
    own_slab = path_delta[0]
    path_count = assign.shape[0]
    module_count, _, own_rows, width = params.shape
    shards = lax.axis_size("shard")
    entries = float(own_slab.size * shards)
    state_in = params.reshape(module_count, own_rows, width)
    moment_in = momentum.reshape(module_count, own_rows, width)
    split_slab = own_slab.reshape(LEVELS, path_count, own_rows, width)
    here = lax.axis_index("path").astype(jnp.int32).reshape(1)
    rows_shape = jax.ShapeDtypeStruct((LEVELS, own_rows, width), jnp.float32)

    squares = call(squares_kernel, jax.ShapeDtypeStruct((8, 128), jnp.float32), [vmem], vmem)(own_slab)
    tiles = exchange([squares] * shards, "shard")
    packed = call(
        lambda *refs: pack_kernel(entries, shards, *refs),
        [rows_shape] * path_count,
        [smem, vmem] + [vmem] * shards,
        [vmem] * path_count,
    )(here, split_slab, *tiles)
    received = exchange(packed, "path")
    base = call(
        gather_kernel,
        jax.ShapeDtypeStruct((LEVELS, path_count, own_rows, width), jnp.float32),
        [smem, smem, anywhere, anywhere],
        vmem,
        scratch_shapes=[
            pltpu.VMEM((LEVELS, path_count, own_rows, width), jnp.float32),
            pltpu.VMEM((LEVELS, path_count, own_rows, width), jnp.float32),
            pltpu.SemaphoreType.DMA((2, LEVELS, path_count)),
        ],
    )(here, assign, state_in, moment_in)
    outgoing = call(
        lambda *refs: outgoing_kernel(path_count, *refs),
        [rows_shape] * path_count,
        [smem, smem, vmem] + [vmem] * path_count,
        [vmem] * path_count,
    )(here, assign, base, *received)
    returned = exchange(outgoing, "path")
    block = LEVEL_MODULES // 4
    state_block = pl.BlockSpec((block, own_rows, width), lambda i: (i, 0, 0))
    new_state, new_moment = call(
        lambda *refs: state_kernel(path_count, *refs),
        [jax.ShapeDtypeStruct(state_in.shape, jnp.float32)] * 2,
        [smem, smem] + [vmem] * path_count + [state_block, state_block],
        [state_block, state_block],
        grid=(module_count // block,),
    )(here, assign, *received, state_in, moment_in)
    path_params = call(
        lambda *refs: assemble_kernel(path_count, *refs),
        jax.ShapeDtypeStruct(split_slab.shape, jnp.float32),
        [smem] + [anywhere] * path_count,
        anywhere,
        scratch_shapes=[pltpu.SemaphoreType.DMA((path_count,))],
    )(here, *returned)
    return (path_params.reshape(path_delta.shape), new_state[:, None], new_moment[:, None])


def solution(mesh):
    in_specs = (
        P("path", None, "shard", None),
        P(),
        P(None, "shard", "path", None),
        P(None, "shard", "path", None),
    )
    out_specs = (
        P("path", None, "shard", None),
        P(None, "shard", "path", None),
        P(None, "shard", "path", None),
    )
    return jax.shard_map(local, mesh=mesh, in_specs=in_specs, out_specs=out_specs, check_vma=False)
```

time: 194 us -> 48.2 us (0.25)
  waiting for transfers between devices: 124 us -> 9.94 us
  starting transfers between devices: 3.6 us -> 20 us
  blocking collectives: 14.1 us -> 0 us
  between operations: 14.8 us -> 0.71 us
  matrix products: 13.1 us -> 0 us
  other arithmetic: 12.5 us -> 0 us
  Pallas kernels: 0 us -> 12.4 us
  local copies, waits for them, and re-layouts: 11.2 us -> 4.95 us
    reduce_scatter x1 -> x0, waiting for transfers between devices: 114 us -> none  [local(): lax.psum_scatter(jnp.einsum('lm,lrd->rmd', own_members, scaled, precision...]
    ppermute x0 -> x17, starting transfers between devices: none -> 20 us  [exchange(): lax.ppermute(arrays[k], axis, [(i, i ^ k) for i in range(size)])]
    psum x1 -> x0, blocking collectives: 14.1 us -> none  [local(): total_sq = lax.psum(squares, 'shard')]
    dot_general x1 -> x0, matrix products: 13.1 us -> none  [local(): jnp.einsum('lm,lrd->rmd', own_members, scaled, precision=lax.Precision.HI...]
    pallas_call x0 -> x6, Pallas kernels: none -> 12.4 us  [the longest x1 5.18 us: local(): call(lambda *refs: state_kernel(path_count, *refs), [jax.ShapeDtypeStruct...]
    all_to_all x1 -> x0, waiting for transfers between devices: 10.3 us -> none  [local(): lax.all_to_all(outgoing, 'path', split_axis=0, concat_axis=2, tiled=True)[0]]
    ppermute x0 -> x17, waiting for transfers between devices: none -> 9.94 us  [exchange(): lax.ppermute(arrays[k], axis, [(i, i ^ k) for i in range(size)])]
    broadcast_in_dim x1 -> x0, other arithmetic: 7.07 us -> none  [local(): return (returned[None], new_state[:, None], new_moment[:, None])]
  transfers between devices with their start and end apart: 2 -> 17, of which waited for: 2 -> 6; matrix products, arithmetic and copies ran while one was open for 3% -> 2% of each run, Pallas kernels for 0% -> 19%
where the time goes in v2:
time: 48.2 us; the launch traced here: 48 us
  starting transfers between devices  20 us (41%)
  Pallas kernels  12.4 us (26%)
  waiting for transfers between devices  9.94 us (21%)
  local copies, waits for them, and re-layouts  4.95 us (10%)
  between operations  0.71 us (1%)
    ppermute x17, starting transfers between devices, exchange(): lax.ppermute(arrays[k], axis, [(i, i ^ k) for i in range(size)])  20 us
    ppermute x17, waiting for transfers between devices, exchange(): lax.ppermute(arrays[k], axis, [(i, i ^ k) for i in range(size)])  9.94 us
    pallas_call x1, Pallas kernels, local(): call(lambda *refs: state_kernel(path_count, *refs), [jax.ShapeDtypeStruct...  5.18 us
    unnamed x11, local copies, waits for them, and re-layouts  4.95 us
    pallas_call x1, Pallas kernels, local(): call(gather_kernel, jax.ShapeDtypeStruct((LEVELS, path_count, own_rows, w...  3.83 us
    pallas_call x1, Pallas kernels, local(): call(lambda *refs: outgoing_kernel(path_count, *refs), [rows_shape] * pat...  1.41 us
    pallas_call x1, Pallas kernels, local(): call(lambda *refs: assemble_kernel(path_count, *refs), jax.ShapeDtypeStru...  1.03 us
  transfers between devices with their start and end apart: 17, of which 6 were waited for; matrix products, arithmetic and copies ran while one was open for 2% of the time, Pallas kernels for 19%

profile of v2, /device:TPU:0, one launch (start us, length us, event | category | flops | bytes accessed | tf_op | source)
XLA Modules:
  0.0 48.0 jit_solution(14365277572219723513)
XLA Ops:
  0.6 0.0 copy-start
  0.6 0.0 copy-start.3
  0.7 1.4 %copy-done.3 = f32[1,2,128,1024]{3,2,1,0:T(8,128)S(1)} copy-done((f32[1,2,128,1024]{3,2,1,0:T(8,128)S(1)}, f32[1,2,128,1024]{3,2,1,0:T(8,128)}, u32[]{:S(2)}) %copy-start.3) | copy-done | bytes 1048600
  2.0 0.1 shard_map.68.refs_2_
  2.1 5.1 %collective-permute-start.2 = (f32[8,128]{1,0:T(8,128)S(1)}, f32[8,128]{1,0:T(8,128)S(1)}, u32[]{:S(2)}, u32[]{:S(2)}) collective-permute-start(f32[8,128]{1,0:T(8,128)S(1)} %shard_map.68.refs_2_), channel_id=1, source_target_pairs={{0,3},{1,2},{2,1},{3,0},{4,7},{5,6},{6,5},{7,4},{8,11},{9,10},{10,... | collective-permute-start | bytes 12296 | tf_op jit(solution)/shard_map/ppermute | solution.py:37
  7.2 0.0 collective-permute-start.1
  7.2 0.6 %collective-permute-start = (f32[8,128]{1,0:T(8,128)S(1)}, f32[8,128]{1,0:T(8,128)S(1)}, u32[]{:S(2)}, u32[]{:S(2)}) collective-permute-start(f32[8,128]{1,0:T(8,128)S(1)} %shard_map.68.refs_2_), channel_id=1, source_target_pairs={{0,1},{1,0},{2,3},{3,2},{4,5},{5,4},{6,7},{7,6},{8,9},{9,8},{10,11... | collective-permute-start | bytes 12296 | tf_op jit(solution)/shard_map/ppermute | solution.py:37
  7.9 0.9 %collective-permute-done.2.refs_5_ = f32[8,128]{1,0:T(8,128)S(1)} collective-permute-done((f32[8,128]{1,0:T(8,128)S(1)}, f32[8,128]{1,0:T(8,128)S(1)}, u32[]{:S(2)}, u32[]{:S(2)}) %collective-permute-start.2) | collective-permute-done | bytes 4128 | tf_op jit(solution)/shard_map/ppermute | solution.py:37
  8.8 2.9 %collective-permute-done.1.refs_4_ = f32[8,128]{1,0:T(8,128)S(1)} collective-permute-done((f32[8,128]{1,0:T(8,128)S(1)}, f32[8,128]{1,0:T(8,128)S(1)}, u32[]{:S(2)}, u32[]{:S(2)}) %collective-permute-start.1) | collective-permute-done | bytes 4128 | tf_op jit(solution)/shard_map/ppermute | solution.py:37
  11.7 0.0 collective-permute-done.refs_3_
  11.7 1.2 %copy-done.4 = f32[1,2,128,1024]{3,2,1,0:T(8,128)S(1)} copy-done((f32[1,2,128,1024]{3,2,1,0:T(8,128)S(1)}, f32[1,2,128,1024]{3,2,1,0:T(8,128)}, u32[]{:S(2)}) %copy-start.4) | copy-done | bytes 1048600
  13.0 0.9 %shard_map.69 = (f32[2,16,1024]{2,1,0:T(8,128)S(1)}, f32[2,16,1024]{2,1,0:T(8,128)S(1)}, f32[2,16,1024]{2,1,0:T(8,128)S(1)}, f32[2,16,1024]{2,1,0:T(8,128)}, f32...) custom-call(s32[1]{0:T(128)} %bitcast.here_ref.refs_0_, ...), custom_call_target="tpu_custom_call" | custom-call | tf_op jit(solution)/shard_map/pallas_call | solution.py:151
  13.8 0.0 collective-permute-start.3
  13.8 1.5 %collective-permute-start.4 = (f32[2,16,1024]{2,1,0:T(8,128)S(1)}, f32[2,16,1024]{2,1,0:T(8,128)S(1)}, u32[]{:S(2)}, u32[]{:S(2)}) collective-permute-start(f32[2,16,1024]{2,1,0:T(8,128)S(1)} %get-tuple-element.23), channel_id=1, source_target_pairs={{0,8},{4,12},{8,0},{12,4},{16,24},{20,28},{24,16},{28,20},{1,9},{5... | collective-permute-start | bytes 393224 | tf_op jit(solution)/shard_map/ppermute | solution.py:37
  15.3 0.4 collective-permute-start.5
  15.7 1.5 %collective-permute-start.6 = (f32[2,16,1024]{2,1,0:T(8,128)}, f32[2,16,1024]{2,1,0:T(8,128)S(1)}, u32[]{:S(2)}, u32[]{:S(2)}) collective-permute-start(f32[2,16,1024]{2,1,0:T(8,128)} %get-tuple-element.25), channel_id=1, source_target_pairs={{0,16},{4,20},{8,24},{12,28},{16,0},{20,4},{24,8},{28,12},{1,17},{... | collective-permute-start | bytes 393224 | tf_op jit(solution)/shard_map/ppermute | solution.py:37
  17.2 0.1 collective-permute-start.7
  17.3 0.0 collective-permute-done.3.refs_4_.refs_3_
  17.3 2.4 %collective-permute-start.8 = (f32[2,16,1024]{2,1,0:T(8,128)S(1)}, f32[2,16,1024]{2,1,0:T(8,128)S(1)}, u32[]{:S(2)}, u32[]{:S(2)}) collective-permute-start(f32[2,16,1024]{2,1,0:T(8,128)S(1)} %get-tuple-element.27), channel_id=1, source_target_pairs={{0,24},{4,28},{8,16},{12,20},{16,8},{20,12},{24,0},{28,4},{1,25},{... | collective-permute-start | bytes 393224 | tf_op jit(solution)/shard_map/ppermute | solution.py:37
  19.8 0.3 collective-permute-done.4.refs_5_.refs_4_
  20.1 1.4 %collective-permute-start.9 = (f32[2,16,1024]{2,1,0:T(8,128)S(1)}, f32[2,16,1024]{2,1,0:T(8,128)S(1)}, u32[]{:S(2)}, u32[]{:S(2)}) collective-permute-start(f32[2,16,1024]{2,1,0:T(8,128)S(1)} %get-tuple-element.28), channel_id=1, source_target_pairs={{0,28},{4,24},{8,20},{12,16},{16,12},{20,8},{24,4},{28,0},{1,29},{... | collective-permute-start | bytes 393224 | tf_op jit(solution)/shard_map/ppermute | solution.py:37
  21.5 0.8 %copy.8.ids_ref.refs_1_ = s32[8,2]{1,0:T(8,128)S(1)} copy(s32[8,2]{0,1:T(2,128)} %param.5) | data formatting | bytes 128 | tf_op args[1]
  22.3 0.0 copy-done
  22.3 1.6 %copy-done.1 = f32[32,1,16,1024]{3,2,1,0:T(8,128)S(1)} copy-done((f32[32,1,16,1024]{3,2,1,0:T(8,128)S(1)}, f32[32,1,16,1024]{3,2,1,0:T(8,128)}, u32[]{:S(2)}) %copy-start.1) | copy-done | bytes 2097176
  23.9 3.8 %shard_map.67.refs_2_ = f32[2,8,16,1024]{3,2,1,0:T(8,128)S(1)} custom-call(s32[1]{0:T(128)} %bitcast.here_ref.refs_0_, s32[8,2]{1,0:T(8,128)S(1)} %copy.8.ids_ref.refs_1_, f32[32,16,1024]{2,1,0:T(8,128)S(1)} %bitcast.12, f32[32,16,1024]{2,1,0:T(8,128)S(1)} %bitcast.14), custom_call_target="tpu_custom_call" | custom-call | tf_op jit(solution)/shard_map/pallas_call | solution.py:158
  27.7 0.0 copy-start.2
  27.7 0.0 collective-permute-done.5.refs_6_.refs_5_
  27.7 0.0 collective-permute-done.6.refs_7_.refs_6_
  27.7 1.6 %collective-permute-done.7.refs_8_.refs_7_ = f32[2,16,1024]{2,1,0:T(8,128)S(1)} collective-permute-done((f32[2,16,1024]{2,1,0:T(8,128)S(1)}, f32[2,16,1024]{2,1,0:T(8,128)S(1)}, u32[]{:S(2)}, u32[]{:S(2)}) %collective-permute-start.7) | collective-permute-done | bytes 131104 | tf_op jit(solution)/shard_map/ppermute | solution.py:37
  29.4 0.0 collective-permute-done.8.refs_9_.refs_8_
  29.4 0.0 collective-permute-done.9.refs_10_.refs_9_
  29.4 1.4 %shard_map.70 = (f32[2,16,1024]{2,1,0:T(8,128)S(1)}, f32[2,16,1024]{2,1,0:T(8,128)S(1)}, f32[2,16,1024]{2,1,0:T(8,128)S(1)}, f32[2,16,1024]{2,1,0:T(8,128)S(1)},...) custom-call(s32[1]{0:T(128)} %bitcast.here_ref.refs_0_, ...), custom_call_target="tpu_custom_call" | custom-call | tf_op jit(solution)/shard_map/pallas_call | solution.py:169
  30.8 0.5 %collective-permute-start.10 = (f32[2,16,1024]{2,1,0:T(8,128)S(1)}, f32[2,16,1024]{2,1,0:T(8,128)S(1)}, u32[]{:S(2)}, u32[]{:S(2)}) collective-permute-start(f32[2,16,1024]{2,1,0:T(8,128)S(1)} %get-tuple-element.30), channel_id=1, source_target_pairs={{0,4},{4,0},{8,12},{12,8},{16,20},{20,16},{24,28},{28,24},{1,5},{5... | collective-permute-start | bytes 393224 | tf_op jit(solution)/shard_map/ppermute | solution.py:37
  31.3 1.5 %collective-permute-start.11 = (f32[2,16,1024]{2,1,0:T(8,128)S(1)}, f32[2,16,1024]{2,1,0:T(8,128)S(1)}, u32[]{:S(2)}, u32[]{:S(2)}) collective-permute-start(f32[2,16,1024]{2,1,0:T(8,128)S(1)} %get-tuple-element.31), channel_id=1, source_target_pairs={{0,8},{4,12},{8,0},{12,4},{16,24},{20,28},{24,16},{28,20},{1,9},{5... | collective-permute-start | bytes 393224 | tf_op jit(solution)/shard_map/ppermute | solution.py:37
  32.8 0.0 collective-permute-start.12
  32.8 1.5 %collective-permute-start.13 = (f32[2,16,1024]{2,1,0:T(8,128)S(1)}, f32[2,16,1024]{2,1,0:T(8,128)S(1)}, u32[]{:S(2)}, u32[]{:S(2)}) collective-permute-start(f32[2,16,1024]{2,1,0:T(8,128)S(1)} %get-tuple-element.33), channel_id=1, source_target_pairs={{0,16},{4,20},{8,24},{12,28},{16,0},{20,4},{24,8},{28,12},{1,17},{... | collective-permute-start | bytes 393224 | tf_op jit(solution)/shard_map/ppermute | solution.py:37
  34.3 0.5 collective-permute-start.14
  34.8 0.0 collective-permute-done.10.refs_2_
  34.8 2.5 %collective-permute-start.15 = (f32[2,16,1024]{2,1,0:T(8,128)S(1)}, f32[2,16,1024]{2,1,0:T(8,128)S(1)}, u32[]{:S(2)}, u32[]{:S(2)}) collective-permute-start(f32[2,16,1024]{2,1,0:T(8,128)S(1)} %get-tuple-element.35), channel_id=1, source_target_pairs={{0,24},{4,28},{8,16},{12,20},{16,8},{20,12},{24,0},{28,4},{1,25},{... | collective-permute-start | bytes 393224 | tf_op jit(solution)/shard_map/ppermute | solution.py:37
  37.3 0.4 collective-permute-done.11.refs_3_
  37.7 0.4 collective-permute-start.16
  38.1 5.2 %shard_map.72 = (f32[32,16,1024]{2,1,0:T(8,128)}, f32[32,16,1024]{2,1,0:T(8,128)}) custom-call(s32[1]{0:T(128)} %bitcast.here_ref.refs_0_, s32[8,2]{1,0:T(8,128)S(1)} %copy.8.ids_ref.refs_1_, f32[2,16,1024]{2,1,0:T(8,128)S(1)} %get-tuple-element.21.refs_3_.refs_2_, f32[2,16,1024]{2,1,0:T(8,128)S(1)} %collective-permute-done.3.refs_4_.refs_3_, ...), custom_call_target="tpu_custom_call" | custom-call | tf_op jit(solution)/shard_map/pallas_call | solution.py:178
  43.3 0.0 collective-permute-done.12.refs_4_
  43.3 0.0 collective-permute-done.13.refs_5_
  43.3 3.7 %collective-permute-done.14.refs_6_ = f32[2,16,1024]{2,1,0:T(8,128)S(1)} collective-permute-done((f32[2,16,1024]{2,1,0:T(8,128)S(1)}, f32[2,16,1024]{2,1,0:T(8,128)S(1)}, u32[]{:S(2)}, u32[]{:S(2)}) %collective-permute-start.14) | collective-permute-done | bytes 131104 | tf_op jit(solution)/shard_map/ppermute | solution.py:37
  47.0 0.0 collective-permute-done.15.refs_7_
  47.0 0.0 collective-permute-done.16.refs_8_
  47.0 1.0 %shard_map.71 = f32[2,8,16,1024]{3,2,1,0:T(8,128)} custom-call(s32[1]{0:T(128)} %bitcast.here_ref.refs_0_, f32[2,16,1024]{2,1,0:T(8,128)S(1)} %get-tuple-element.29.refs_1_, f32[2,16,1024]{2,1,0:T(8,128)S(1)} %collective-permute-done.10.refs_2_, f32[2,16,1024]{2,1,0:T(8,128)S(1)} %collective-permute-done.11.refs_3_, ...), custom_call_target="tpu_custom_call" | custom-call | tf_op jit(solution)/shard_map/pallas_call | solution.py:185
  (3 shorter events, 0.0 us)
Async XLA Ops:
  0.6 21.6 %copy-start = (f32[32,1,16,1024]{3,2,1,0:T(8,128)S(1)}, f32[32,1,16,1024]{3,2,1,0:T(8,128)}, u32[]{:S(2)}) copy-start(f32[32,1,16,1024]{3,2,1,0:T(8,128)} %param.6) | copy-start | bytes 6291460
  0.6 1.4 %copy-start.3 = (f32[1,2,128,1024]{3,2,1,0:T(8,128)S(1)}, f32[1,2,128,1024]{3,2,1,0:T(8,128)}, u32[]{:S(2)}) copy-start(f32[1,2,128,1024]{3,2,1,0:T(8,128)} %param.4) | copy-start | bytes 3145732
  2.1 6.7 %collective-permute-start.2 = (f32[8,128]{1,0:T(8,128)S(1)}, f32[8,128]{1,0:T(8,128)S(1)}, u32[]{:S(2)}, u32[]{:S(2)}) collective-permute-start(f32[8,128]{1,0:T(8,128)S(1)} %shard_map.68.refs_2_), channel_id=1, source_target_pairs={{0,3},{1,2},{2,1},{3,0},{4,7},{5,6},{6,5},{7,4},{8,11},{9,10},{10,... | collective-permute-start | bytes 12296 | tf_op jit(solution)/shard_map/ppermute | solution.py:37
  7.2 4.5 %collective-permute-start.1 = (f32[8,128]{1,0:T(8,128)S(1)}, f32[8,128]{1,0:T(8,128)S(1)}, u32[]{:S(2)}, u32[]{:S(2)}) collective-permute-start(f32[8,128]{1,0:T(8,128)S(1)} %shard_map.68.refs_2_), channel_id=1, source_target_pairs={{0,2},{1,3},{2,0},{3,1},{4,6},{5,7},{6,4},{7,5},{8,10},{9,11},{10,... | collective-permute-start | bytes 12296 | tf_op jit(solution)/shard_map/ppermute | solution.py:37
  7.2 4.5 %collective-permute-start = (f32[8,128]{1,0:T(8,128)S(1)}, f32[8,128]{1,0:T(8,128)S(1)}, u32[]{:S(2)}, u32[]{:S(2)}) collective-permute-start(f32[8,128]{1,0:T(8,128)S(1)} %shard_map.68.refs_2_), channel_id=1, source_target_pairs={{0,1},{1,0},{2,3},{3,2},{4,5},{5,4},{6,7},{7,6},{8,9},{9,8},{10,11... | collective-permute-start | bytes 12296 | tf_op jit(solution)/shard_map/ppermute | solution.py:37
  11.7 1.2 %copy-start.4 = (f32[1,2,128,1024]{3,2,1,0:T(8,128)S(1)}, f32[1,2,128,1024]{3,2,1,0:T(8,128)}, u32[]{:S(2)}) copy-start(f32[1,2,128,1024]{3,2,1,0:T(8,128)} %param.4) | copy-start | bytes 3145732
  13.8 3.5 %collective-permute-start.3 = (f32[2,16,1024]{2,1,0:T(8,128)S(1)}, f32[2,16,1024]{2,1,0:T(8,128)S(1)}, u32[]{:S(2)}, u32[]{:S(2)}) collective-permute-start(f32[2,16,1024]{2,1,0:T(8,128)S(1)} %get-tuple-element.22), channel_id=1, source_target_pairs={{0,4},{4,0},{8,12},{12,8},{16,20},{20,16},{24,28},{28,24},{1,5},{5... | collective-permute-start | bytes 393224 | tf_op jit(solution)/shard_map/ppermute | solution.py:37
  13.8 6.3 %collective-permute-start.4 = (f32[2,16,1024]{2,1,0:T(8,128)S(1)}, f32[2,16,1024]{2,1,0:T(8,128)S(1)}, u32[]{:S(2)}, u32[]{:S(2)}) collective-permute-start(f32[2,16,1024]{2,1,0:T(8,128)S(1)} %get-tuple-element.23), channel_id=1, source_target_pairs={{0,8},{4,12},{8,0},{12,4},{16,24},{20,28},{24,16},{28,20},{1,9},{5... | collective-permute-start | bytes 393224 | tf_op jit(solution)/shard_map/ppermute | solution.py:37
  15.3 12.4 %collective-permute-start.5 = (f32[2,16,1024]{2,1,0:T(8,128)}, f32[2,16,1024]{2,1,0:T(8,128)S(1)}, u32[]{:S(2)}, u32[]{:S(2)}) collective-permute-start(f32[2,16,1024]{2,1,0:T(8,128)} %get-tuple-element.24), channel_id=1, source_target_pairs={{0,12},{4,8},{8,4},{12,0},{16,28},{20,24},{24,20},{28,16},{1,13},{... | collective-permute-start | bytes 393224 | tf_op jit(solution)/shard_map/ppermute | solution.py:37
  15.7 12.0 %collective-permute-start.6 = (f32[2,16,1024]{2,1,0:T(8,128)}, f32[2,16,1024]{2,1,0:T(8,128)S(1)}, u32[]{:S(2)}, u32[]{:S(2)}) collective-permute-start(f32[2,16,1024]{2,1,0:T(8,128)} %get-tuple-element.25), channel_id=1, source_target_pairs={{0,16},{4,20},{8,24},{12,28},{16,0},{20,4},{24,8},{28,12},{1,17},{... | collective-permute-start | bytes 393224 | tf_op jit(solution)/shard_map/ppermute | solution.py:37
  17.2 12.2 %collective-permute-start.7 = (f32[2,16,1024]{2,1,0:T(8,128)S(1)}, f32[2,16,1024]{2,1,0:T(8,128)S(1)}, u32[]{:S(2)}, u32[]{:S(2)}) collective-permute-start(f32[2,16,1024]{2,1,0:T(8,128)S(1)} %get-tuple-element.26), channel_id=1, source_target_pairs={{0,20},{4,16},{8,28},{12,24},{16,4},{20,0},{24,12},{28,8},{1,21},{... | collective-permute-start | bytes 393224 | tf_op jit(solution)/shard_map/ppermute | solution.py:37
  17.3 12.0 %collective-permute-start.8 = (f32[2,16,1024]{2,1,0:T(8,128)S(1)}, f32[2,16,1024]{2,1,0:T(8,128)S(1)}, u32[]{:S(2)}, u32[]{:S(2)}) collective-permute-start(f32[2,16,1024]{2,1,0:T(8,128)S(1)} %get-tuple-element.27), channel_id=1, source_target_pairs={{0,24},{4,28},{8,16},{12,20},{16,8},{20,12},{24,0},{28,4},{1,25},{... | collective-permute-start | bytes 393224 | tf_op jit(solution)/shard_map/ppermute | solution.py:37
  20.1 9.2 %collective-permute-start.9 = (f32[2,16,1024]{2,1,0:T(8,128)S(1)}, f32[2,16,1024]{2,1,0:T(8,128)S(1)}, u32[]{:S(2)}, u32[]{:S(2)}) collective-permute-start(f32[2,16,1024]{2,1,0:T(8,128)S(1)} %get-tuple-element.28), channel_id=1, source_target_pairs={{0,28},{4,24},{8,20},{12,16},{16,12},{20,8},{24,4},{28,0},{1,29},{... | collective-permute-start | bytes 393224 | tf_op jit(solution)/shard_map/ppermute | solution.py:37
  22.3 1.6 %copy-start.1 = (f32[32,1,16,1024]{3,2,1,0:T(8,128)S(1)}, f32[32,1,16,1024]{3,2,1,0:T(8,128)}, u32[]{:S(2)}) copy-start(f32[32,1,16,1024]{3,2,1,0:T(8,128)} %param.7) | copy-start | bytes 6291460
  27.7 10.4 %copy-start.2 = (f32[32,1,16,1024]{3,2,1,0:T(8,128)S(1)}, f32[32,1,16,1024]{3,2,1,0:T(8,128)}, u32[]{:S(2)}) copy-start(f32[32,1,16,1024]{3,2,1,0:T(8,128)} %param.7) | copy-start | bytes 6291460
  30.8 4.0 %collective-permute-start.10 = (f32[2,16,1024]{2,1,0:T(8,128)S(1)}, f32[2,16,1024]{2,1,0:T(8,128)S(1)}, u32[]{:S(2)}, u32[]{:S(2)}) collective-permute-start(f32[2,16,1024]{2,1,0:T(8,128)S(1)} %get-tuple-element.30), channel_id=1, source_target_pairs={{0,4},{4,0},{8,12},{12,8},{16,20},{20,16},{24,28},{28,24},{1,5},{5... | collective-permute-start | bytes 393224 | tf_op jit(solution)/shard_map/ppermute | solution.py:37
  31.3 6.4 %collective-permute-start.11 = (f32[2,16,1024]{2,1,0:T(8,128)S(1)}, f32[2,16,1024]{2,1,0:T(8,128)S(1)}, u32[]{:S(2)}, u32[]{:S(2)}) collective-permute-start(f32[2,16,1024]{2,1,0:T(8,128)S(1)} %get-tuple-element.31), channel_id=1, source_target_pairs={{0,8},{4,12},{8,0},{12,4},{16,24},{20,28},{24,16},{28,20},{1,9},{5... | collective-permute-start | bytes 393224 | tf_op jit(solution)/shard_map/ppermute | solution.py:37
  32.8 10.5 %collective-permute-start.12 = (f32[2,16,1024]{2,1,0:T(8,128)S(1)}, f32[2,16,1024]{2,1,0:T(8,128)S(1)}, u32[]{:S(2)}, u32[]{:S(2)}) collective-permute-start(f32[2,16,1024]{2,1,0:T(8,128)S(1)} %get-tuple-element.32), channel_id=1, source_target_pairs={{0,12},{4,8},{8,4},{12,0},{16,28},{20,24},{24,20},{28,16},{1,13},{... | collective-permute-start | bytes 393224 | tf_op jit(solution)/shard_map/ppermute | solution.py:37
  32.8 10.5 %collective-permute-start.13 = (f32[2,16,1024]{2,1,0:T(8,128)S(1)}, f32[2,16,1024]{2,1,0:T(8,128)S(1)}, u32[]{:S(2)}, u32[]{:S(2)}) collective-permute-start(f32[2,16,1024]{2,1,0:T(8,128)S(1)} %get-tuple-element.33), channel_id=1, source_target_pairs={{0,16},{4,20},{8,24},{12,28},{16,0},{20,4},{24,8},{28,12},{1,17},{... | collective-permute-start | bytes 393224 | tf_op jit(solution)/shard_map/ppermute | solution.py:37
  34.3 12.6 %collective-permute-start.14 = (f32[2,16,1024]{2,1,0:T(8,128)S(1)}, f32[2,16,1024]{2,1,0:T(8,128)S(1)}, u32[]{:S(2)}, u32[]{:S(2)}) collective-permute-start(f32[2,16,1024]{2,1,0:T(8,128)S(1)} %get-tuple-element.34), channel_id=1, source_target_pairs={{0,20},{4,16},{8,28},{12,24},{16,4},{20,0},{24,12},{28,8},{1,21},{... | collective-permute-start | bytes 393224 | tf_op jit(solution)/shard_map/ppermute | solution.py:37
  34.8 12.2 %collective-permute-start.15 = (f32[2,16,1024]{2,1,0:T(8,128)S(1)}, f32[2,16,1024]{2,1,0:T(8,128)S(1)}, u32[]{:S(2)}, u32[]{:S(2)}) collective-permute-start(f32[2,16,1024]{2,1,0:T(8,128)S(1)} %get-tuple-element.35), channel_id=1, source_target_pairs={{0,24},{4,28},{8,16},{12,20},{16,8},{20,12},{24,0},{28,4},{1,25},{... | collective-permute-start | bytes 393224 | tf_op jit(solution)/shard_map/ppermute | solution.py:37
  37.7 9.3 %collective-permute-start.16 = (f32[2,16,1024]{2,1,0:T(8,128)S(1)}, f32[2,16,1024]{2,1,0:T(8,128)S(1)}, u32[]{:S(2)}, u32[]{:S(2)}) collective-permute-start(f32[2,16,1024]{2,1,0:T(8,128)S(1)} %get-tuple-element.36), channel_id=1, source_target_pairs={{0,28},{4,24},{8,20},{12,16},{16,12},{20,8},{24,4},{28,0},{1,29},{... | collective-permute-start | bytes 393224 | tf_op jit(solution)/shard_map/ppermute | solution.py:37

commit v3 on v2

--- a/solution.py
+++ b/solution.py
@@ -7,13 +7,14 @@
 
 LEVEL_MODULES = 16
 LEVELS = 2
+MOST_UNROLLED = 16
 
 outer_rate = 0.7
 beta_coef = 0.9
 moment_coef = outer_rate * beta_coef * beta_coef
 grad_coef = outer_rate * (1.0 + beta_coef)
 
-VMEM_LIMIT = 48 * 1024 * 1024
+VMEM_LIMIT = 16 * 1024 * 1024
 
 vmem = pl.BlockSpec(memory_space=pltpu.VMEM)
 smem = pl.BlockSpec(memory_space=pltpu.SMEM)
@@ -31,11 +32,31 @@
     )
 
 
-def exchange(arrays, axis):
-    size = lax.axis_size(axis)
-    return [arrays[0]] + [
-        lax.ppermute(arrays[k], axis, [(i, i ^ k) for i in range(size)]) for k in range(1, size)
-    ]
+def mirrored(k, size):
+    if size < 8:
+        return k
+    return (k & ~6) | ((k & 2) << 1) | ((k & 4) >> 1)
+
+
+def target(here, k, size):
+    if isinstance(here, int):
+        return here ^ (mirrored(k, size) if here & 1 else k)
+    return here ^ jnp.where(here & 1 == 1, mirrored(k, size), k)
+
+
+def origin(here, k, size):
+    if isinstance(here, int):
+        return here ^ (mirrored(k, size) if (here ^ k) & 1 else k)
+    return here ^ jnp.where((here ^ k) & 1 == 1, mirrored(k, size), k)
+
+
+def exchange(arrays):
+    size = len(arrays)
+    moved = dict(enumerate(arrays))
+    first = [1, 6, 7, 2, 4, 3, 5] if size == 8 else list(range(1, size))
+    for k in first:
+        moved[k] = lax.ppermute(arrays[k], "path", [(i, target(i, k, size)) for i in range(size)])
+    return [moved[k] for k in range(size)]
 
 
 def squares_kernel(delta_ref, out_ref):
@@ -56,8 +77,9 @@
         tile = tile + other[...]
     rescale = 1.0 / jnp.sqrt(jnp.sum(tile, keepdims=True) / entries + 1e-06)
     for k, out in enumerate(outs):
+        place = target(here_ref[0], k, len(outs))
         for level in range(LEVELS):
-            out[level] = delta_ref[level, here_ref[0] ^ k] * rescale
+            out[level] = delta_ref[level, place] * rescale
 
 
 def gather_kernel(here_ref, ids_ref, params_ref, momentum_ref, out_ref, param_rows, moment_rows, sems):
@@ -65,7 +87,7 @@
     copies = []
     for level in range(LEVELS):
         for k in range(path_count):
-            module = ids_ref[here_ref[0] ^ k, level] + level * LEVEL_MODULES
+            module = ids_ref[target(here_ref[0], k, path_count), level] + level * LEVEL_MODULES
             copies.append(
                 (
                     pltpu.make_async_copy(params_ref.at[module], param_rows.at[level, k], sems.at[0, level, k]),
@@ -95,11 +117,12 @@
     here = here_ref[0]
     for level in range(LEVELS):
         for k in range(path_count):
-            module = ids_ref[here ^ k, level]
+            module = ids_ref[target(here, k, path_count), level]
             weight = grad_coef / sharers_of(ids_ref, level, module)
             total = base_ref[level, k]
             for other in range(path_count):
-                factor = jnp.where(ids_ref[here ^ other, level] == module, weight, 0.0)
+                owner = origin(here, other, path_count)
+                factor = jnp.where(ids_ref[owner, level] == module, weight, 0.0)
                 total = total - factor * received[other][level]
             outs[k][level] = total
 
@@ -116,7 +139,8 @@
         weight = 1.0 / sharers_of(ids_ref, level, module)
         grad = jnp.zeros(params_ref.shape[1:], jnp.float32)
         for other in range(path_count):
-            factor = jnp.where(ids_ref[here ^ other, level] == module, weight, 0.0)
+            owner = origin(here, other, path_count)
+            factor = jnp.where(ids_ref[owner, level] == module, weight, 0.0)
             grad = grad + factor * received[other][level]
         new_moment = beta_coef * momentum_ref[place] + grad
         new_momentum_ref[place] = new_moment
@@ -127,7 +151,8 @@
     returned, out_ref, sems = refs[:path_count], refs[path_count], refs[path_count + 1]
     copies = []
     for k in range(path_count):
-        copies.append(pltpu.make_async_copy(returned[k], out_ref.at[:, here_ref[0] ^ k], sems.at[k]))
+        place = origin(here_ref[0], k, path_count)
+        copies.append(pltpu.make_async_copy(returned[k], out_ref.at[:, place], sems.at[k]))
     for copy in copies:
         copy.start()
     for copy in copies:
@@ -147,14 +172,17 @@
     rows_shape = jax.ShapeDtypeStruct((LEVELS, own_rows, width), jnp.float32)
 
     squares = call(squares_kernel, jax.ShapeDtypeStruct((8, 128), jnp.float32), [vmem], vmem)(own_slab)
-    tiles = exchange([squares] * shards, "shard")
+    tiles = [squares] + [
+        lax.ppermute(squares, "shard", [(i, (i + step) % shards) for i in range(shards)])
+        for step in range(1, shards)
+    ]
     packed = call(
         lambda *refs: pack_kernel(entries, shards, *refs),
         [rows_shape] * path_count,
         [smem, vmem] + [vmem] * shards,
         [vmem] * path_count,
     )(here, split_slab, *tiles)
-    received = exchange(packed, "path")
+    received = exchange(packed)
     base = call(
         gather_kernel,
         jax.ShapeDtypeStruct((LEVELS, path_count, own_rows, width), jnp.float32),
@@ -172,7 +200,7 @@
         [smem, smem, vmem] + [vmem] * path_count,
         [vmem] * path_count,
     )(here, assign, base, *received)
-    returned = exchange(outgoing, "path")
+    returned = exchange(outgoing)
     block = LEVEL_MODULES // 4
     state_block = pl.BlockSpec((block, own_rows, width), lambda i: (i, 0, 0))
     new_state, new_moment = call(
@@ -192,6 +220,29 @@
     return (path_params.reshape(path_delta.shape), new_state[:, None], new_moment[:, None])
 
 
+def local_wide(path_delta, assign, params, momentum):
+    own_slab = path_delta[0]
+    path_count = assign.shape[0]
+    module_count, _, own_rows, width = params.shape
+    entries = float(own_slab.size * lax.axis_size("shard"))
+    total_sq = lax.psum(jnp.sum(own_slab * own_slab), "shard")
+    scaled = own_slab * (1.0 / jnp.sqrt(total_sq / entries + 1e-06))
+    received = lax.all_to_all(
+        scaled.reshape(LEVELS, path_count, own_rows, width), "path", split_axis=1, concat_axis=1, tiled=True
+    )
+    flat_ids = (assign + LEVEL_MODULES * jnp.arange(LEVELS, dtype=jnp.int32)[None, :]).T.reshape(-1)
+    member = (jnp.arange(module_count, dtype=jnp.int32)[:, None] == flat_ids[None, :]).astype(jnp.float32)
+    mean = member / jnp.maximum(jnp.sum(member, axis=1), 1.0)[:, None]
+    grad = jnp.einsum(
+        "mp,prd->mrd", mean, received.reshape(-1, own_rows, width), precision=lax.Precision.HIGHEST
+    )
+    new_moment = beta_coef * momentum[:, 0] + grad
+    new_state = params[:, 0] - outer_rate * (grad + beta_coef * new_moment)
+    outgoing = jnp.take(new_state, flat_ids, axis=0).reshape(LEVELS, path_count, own_rows, width)
+    returned = lax.all_to_all(outgoing, "path", split_axis=1, concat_axis=1, tiled=True)
+    return (returned.reshape(path_delta.shape), new_state[:, None], new_moment[:, None])
+
+
 def solution(mesh):
     in_specs = (
         P("path", None, "shard", None),
@@ -204,4 +255,5 @@
         P(None, "shard", "path", None),
         P(None, "shard", "path", None),
     )
-    return jax.shard_map(local, mesh=mesh, in_specs=in_specs, out_specs=out_specs, check_vma=False)
+    chosen = local if mesh.shape["path"] <= MOST_UNROLLED else local_wide
+    return jax.shard_map(chosen, mesh=mesh, in_specs=in_specs, out_specs=out_specs, check_vma=False)

time: 48.2 us -> 48.2 us (level)
  starting transfers between devices: 20 us -> 18.8 us
  waiting for transfers between devices: 9.94 us -> 11 us
    ppermute x17, starting transfers between devices: 20 us -> 18.8 us  [the longest x14 12.7 us: exchange(): lax.ppermute(arrays[k], 'path', [(i, target(i, k, size)) for i in range(s...]
    ppermute x17, waiting for transfers between devices: 9.94 us -> 11 us  [the longest x14 6.61 us: exchange(): lax.ppermute(arrays[k], 'path', [(i, target(i, k, size)) for i in range(s...]
where the time goes in v3:
time: 48.2 us; the launch traced here: 48 us
  starting transfers between devices  18.8 us (39%)
  Pallas kernels  12.4 us (26%)
  waiting for transfers between devices  11 us (23%)
  local copies, waits for them, and re-layouts  4.95 us (10%)
  between operations  0.74 us (2%)
    ppermute x14, starting transfers between devices, exchange(): lax.ppermute(arrays[k], 'path', [(i, target(i, k, size)) for i in range(s...  12.7 us
    ppermute x14, waiting for transfers between devices, exchange(): lax.ppermute(arrays[k], 'path', [(i, target(i, k, size)) for i in range(s...  6.61 us
    ppermute x3, starting transfers between devices, local(): lax.ppermute(squares, 'shard', [(i, (i + step) % shards) for i in range(s...  6.11 us
    pallas_call x1, Pallas kernels, local(): call(lambda *refs: state_kernel(path_count, *refs), [jax.ShapeDtypeStruct...  5.2 us
    unnamed x11, local copies, waits for them, and re-layouts  4.95 us
    ppermute x3, waiting for transfers between devices, local(): lax.ppermute(squares, 'shard', [(i, (i + step) % shards) for i in range(s...  4.39 us
    pallas_call x1, Pallas kernels, local(): call(gather_kernel, jax.ShapeDtypeStruct((LEVELS, path_count, own_rows, w...  3.83 us
    pallas_call x1, Pallas kernels, local(): call(lambda *refs: outgoing_kernel(path_count, *refs), [rows_shape] * pat...  1.41 us
  transfers between devices with their start and end apart: 17, of which 6 were waited for; matrix products, arithmetic and copies ran while one was open for 2% of the time, Pallas kernels for 19%

profile of v3, /device:TPU:0, one launch (start us, length us, event | category | flops | bytes accessed | tf_op | source)
XLA Modules:
  0.0 48.0 jit_solution(14712437996058124859)
XLA Ops:
  0.6 0.0 copy-start
  0.6 0.0 copy-start.3
  0.7 1.4 %copy-done.3 = f32[1,2,128,1024]{3,2,1,0:T(8,128)S(1)} copy-done((f32[1,2,128,1024]{3,2,1,0:T(8,128)S(1)}, f32[1,2,128,1024]{3,2,1,0:T(8,128)}, u32[]{:S(2)}) %copy-start.3) | copy-done | bytes 1048600
  2.0 0.1 shard_map.68.refs_2_
  2.1 5.1 %collective-permute-start.2 = (f32[8,128]{1,0:T(8,128)S(1)}, f32[8,128]{1,0:T(8,128)S(1)}, u32[]{:S(2)}, u32[]{:S(2)}) collective-permute-start(f32[8,128]{1,0:T(8,128)S(1)} %shard_map.68.refs_2_), channel_id=1, source_target_pairs={{0,3},{1,0},{2,1},{3,2},{4,7},{5,4},{6,5},{7,6},{8,11},{9,8},{10,9... | collective-permute-start | bytes 12296 | tf_op jit(solution)/shard_map/ppermute | solution.py:176
  7.2 0.0 collective-permute-start.1
  7.2 1.0 %collective-permute-start = (f32[8,128]{1,0:T(8,128)S(1)}, f32[8,128]{1,0:T(8,128)S(1)}, u32[]{:S(2)}, u32[]{:S(2)}) collective-permute-start(f32[8,128]{1,0:T(8,128)S(1)} %shard_map.68.refs_2_), channel_id=1, source_target_pairs={{0,1},{1,2},{2,3},{3,0},{4,5},{5,6},{6,7},{7,4},{8,9},{9,10},{10,1... | collective-permute-start | bytes 12296 | tf_op jit(solution)/shard_map/ppermute | solution.py:176
  8.2 0.3 collective-permute-done.2.refs_5_
  8.5 3.2 %collective-permute-done.1.refs_4_ = f32[8,128]{1,0:T(8,128)S(1)} collective-permute-done((f32[8,128]{1,0:T(8,128)S(1)}, f32[8,128]{1,0:T(8,128)S(1)}, u32[]{:S(2)}, u32[]{:S(2)}) %collective-permute-start.1) | collective-permute-done | bytes 4128 | tf_op jit(solution)/shard_map/ppermute | solution.py:176
  11.7 0.9 %collective-permute-done.refs_3_ = f32[8,128]{1,0:T(8,128)S(1)} collective-permute-done((f32[8,128]{1,0:T(8,128)S(1)}, f32[8,128]{1,0:T(8,128)S(1)}, u32[]{:S(2)}, u32[]{:S(2)}) %collective-permute-start) | collective-permute-done | bytes 4128 | tf_op jit(solution)/shard_map/ppermute | solution.py:176
  12.6 1.2 %copy-done.4 = f32[1,2,128,1024]{3,2,1,0:T(8,128)S(1)} copy-done((f32[1,2,128,1024]{3,2,1,0:T(8,128)S(1)}, f32[1,2,128,1024]{3,2,1,0:T(8,128)}, u32[]{:S(2)}) %copy-start.4) | copy-done | bytes 1048600
  13.8 0.9 %shard_map.69 = (f32[2,16,1024]{2,1,0:T(8,128)S(1)}, f32[2,16,1024]{2,1,0:T(8,128)S(1)}, f32[2,16,1024]{2,1,0:T(8,128)S(1)}, f32[2,16,1024]{2,1,0:T(8,128)}, f32...) custom-call(s32[1]{0:T(128)} %bitcast.here_ref.refs_0_, ...), custom_call_target="tpu_custom_call" | custom-call | tf_op jit(solution)/shard_map/pallas_call | solution.py:179
  14.7 0.0 collective-permute-start.3
  14.7 1.5 %collective-permute-start.4 = (f32[2,16,1024]{2,1,0:T(8,128)S(1)}, f32[2,16,1024]{2,1,0:T(8,128)S(1)}, u32[]{:S(2)}, u32[]{:S(2)}) collective-permute-start(f32[2,16,1024]{2,1,0:T(8,128)S(1)} %get-tuple-element.23), channel_id=1, source_target_pairs={{0,8},{4,20},{8,0},{12,28},{16,24},{20,4},{24,16},{28,12},{1,9},{5... | collective-permute-start | bytes 393224 | tf_op jit(solution)/shard_map/ppermute | solution.py:58
  16.2 1.4 %collective-permute-start.5 = (f32[2,16,1024]{2,1,0:T(8,128)}, f32[2,16,1024]{2,1,0:T(8,128)S(1)}, u32[]{:S(2)}, u32[]{:S(2)}) collective-permute-start(f32[2,16,1024]{2,1,0:T(8,128)} %get-tuple-element.24), channel_id=1, source_target_pairs={{0,12},{4,16},{8,4},{12,24},{16,28},{20,0},{24,20},{28,8},{1,13},{... | collective-permute-start | bytes 393224 | tf_op jit(solution)/shard_map/ppermute | solution.py:58
  17.6 0.5 %collective-permute-start.6 = (f32[2,16,1024]{2,1,0:T(8,128)}, f32[2,16,1024]{2,1,0:T(8,128)S(1)}, u32[]{:S(2)}, u32[]{:S(2)}) collective-permute-start(f32[2,16,1024]{2,1,0:T(8,128)} %get-tuple-element.25), channel_id=1, source_target_pairs={{0,16},{4,12},{8,24},{12,4},{16,0},{20,28},{24,8},{28,20},{1,17},{... | collective-permute-start | bytes 393224 | tf_op jit(solution)/shard_map/ppermute | solution.py:58
  18.1 0.1 collective-permute-start.7
  18.2 0.0 collective-permute-done.3.refs_4_.refs_3_
  18.2 2.4 %collective-permute-start.8 = (f32[2,16,1024]{2,1,0:T(8,128)S(1)}, f32[2,16,1024]{2,1,0:T(8,128)S(1)}, u32[]{:S(2)}, u32[]{:S(2)}) collective-permute-start(f32[2,16,1024]{2,1,0:T(8,128)S(1)} %get-tuple-element.27), channel_id=1, source_target_pairs={{0,24},{4,28},{8,16},{12,20},{16,8},{20,12},{24,0},{28,4},{1,25},{... | collective-permute-start | bytes 393224 | tf_op jit(solution)/shard_map/ppermute | solution.py:58
  20.7 0.0 collective-permute-done.4.refs_5_.refs_4_
  20.7 0.7 %collective-permute-start.9 = (f32[2,16,1024]{2,1,0:T(8,128)S(1)}, f32[2,16,1024]{2,1,0:T(8,128)S(1)}, u32[]{:S(2)}, u32[]{:S(2)}) collective-permute-start(f32[2,16,1024]{2,1,0:T(8,128)S(1)} %get-tuple-element.28), channel_id=1, source_target_pairs={{0,28},{4,24},{8,20},{12,16},{16,12},{20,8},{24,4},{28,0},{1,29},{... | collective-permute-start | bytes 393224 | tf_op jit(solution)/shard_map/ppermute | solution.py:58
  21.4 0.8 %copy.8.ids_ref.refs_1_ = s32[8,2]{1,0:T(8,128)S(1)} copy(s32[8,2]{0,1:T(2,128)} %param.5) | data formatting | bytes 128 | tf_op args[1]
  22.1 1.6 %copy-done.1 = f32[32,1,16,1024]{3,2,1,0:T(8,128)S(1)} copy-done((f32[32,1,16,1024]{3,2,1,0:T(8,128)S(1)}, f32[32,1,16,1024]{3,2,1,0:T(8,128)}, u32[]{:S(2)}) %copy-start.1) | copy-done | bytes 2097176
  23.7 3.8 %shard_map.67.refs_2_ = f32[2,8,16,1024]{3,2,1,0:T(8,128)S(1)} custom-call(s32[1]{0:T(128)} %bitcast.here_ref.refs_0_, s32[8,2]{1,0:T(8,128)S(1)} %copy.8.ids_ref.refs_1_, f32[32,16,1024]{2,1,0:T(8,128)S(1)} %bitcast.12, f32[32,16,1024]{2,1,0:T(8,128)S(1)} %bitcast.14), custom_call_target="tpu_custom_call" | custom-call | tf_op jit(solution)/shard_map/pallas_call | solution.py:186
  27.6 0.0 copy-start.2
  27.6 0.0 collective-permute-done.5.refs_6_.refs_5_
  27.6 0.0 collective-permute-done.6.refs_7_.refs_6_
  27.6 0.0 collective-permute-done.7.refs_8_.refs_7_
  27.6 0.0 collective-permute-done.8.refs_9_.refs_8_
  27.6 2.8 %collective-permute-done.9.refs_10_.refs_9_ = f32[2,16,1024]{2,1,0:T(8,128)S(1)} collective-permute-done((f32[2,16,1024]{2,1,0:T(8,128)S(1)}, f32[2,16,1024]{2,1,0:T(8,128)S(1)}, u32[]{:S(2)}, u32[]{:S(2)}) %collective-permute-start.9) | collective-permute-done | bytes 131104 | tf_op jit(solution)/shard_map/ppermute | solution.py:58
  30.5 1.4 %shard_map.70 = (f32[2,16,1024]{2,1,0:T(8,128)S(1)}, f32[2,16,1024]{2,1,0:T(8,128)S(1)}, f32[2,16,1024]{2,1,0:T(8,128)S(1)}, f32[2,16,1024]{2,1,0:T(8,128)S(1)},...) custom-call(s32[1]{0:T(128)} %bitcast.here_ref.refs_0_, ...), custom_call_target="tpu_custom_call" | custom-call | tf_op jit(solution)/shard_map/pallas_call | solution.py:197
  31.9 0.1 collective-permute-start.10
  32.0 1.6 %collective-permute-start.11 = (f32[2,16,1024]{2,1,0:T(8,128)S(1)}, f32[2,16,1024]{2,1,0:T(8,128)S(1)}, u32[]{:S(2)}, u32[]{:S(2)}) collective-permute-start(f32[2,16,1024]{2,1,0:T(8,128)S(1)} %get-tuple-element.31), channel_id=1, source_target_pairs={{0,8},{4,20},{8,0},{12,28},{16,24},{20,4},{24,16},{28,12},{1,9},{5... | collective-permute-start | bytes 393224 | tf_op jit(solution)/shard_map/ppermute | solution.py:58
  33.5 0.3 collective-permute-start.12
  33.8 1.5 %collective-permute-start.13 = (f32[2,16,1024]{2,1,0:T(8,128)S(1)}, f32[2,16,1024]{2,1,0:T(8,128)S(1)}, u32[]{:S(2)}, u32[]{:S(2)}) collective-permute-start(f32[2,16,1024]{2,1,0:T(8,128)S(1)} %get-tuple-element.33), channel_id=1, source_target_pairs={{0,16},{4,12},{8,24},{12,4},{16,0},{20,28},{24,8},{28,20},{1,17},{... | collective-permute-start | bytes 393224 | tf_op jit(solution)/shard_map/ppermute | solution.py:58
  35.3 0.2 collective-permute-start.14
  35.5 0.0 collective-permute-done.10.refs_2_
  35.5 1.4 %collective-permute-start.15 = (f32[2,16,1024]{2,1,0:T(8,128)S(1)}, f32[2,16,1024]{2,1,0:T(8,128)S(1)}, u32[]{:S(2)}, u32[]{:S(2)}) collective-permute-start(f32[2,16,1024]{2,1,0:T(8,128)S(1)} %get-tuple-element.35), channel_id=1, source_target_pairs={{0,24},{4,28},{8,16},{12,20},{16,8},{20,12},{24,0},{28,4},{1,25},{... | collective-permute-start | bytes 393224 | tf_op jit(solution)/shard_map/ppermute | solution.py:58
  37.0 0.3 collective-permute-done.11.refs_3_
  37.2 1.0 %collective-permute-start.16 = (f32[2,16,1024]{2,1,0:T(8,128)S(1)}, f32[2,16,1024]{2,1,0:T(8,128)S(1)}, u32[]{:S(2)}, u32[]{:S(2)}) collective-permute-start(f32[2,16,1024]{2,1,0:T(8,128)S(1)} %get-tuple-element.36), channel_id=1, source_target_pairs={{0,28},{4,24},{8,20},{12,16},{16,12},{20,8},{24,4},{28,0},{1,29},{... | collective-permute-start | bytes 393224 | tf_op jit(solution)/shard_map/ppermute | solution.py:58
  38.2 0.0 copy-done.2
  38.2 5.2 %shard_map.72 = (f32[32,16,1024]{2,1,0:T(8,128)}, f32[32,16,1024]{2,1,0:T(8,128)}) custom-call(s32[1]{0:T(128)} %bitcast.here_ref.refs_0_, s32[8,2]{1,0:T(8,128)S(1)} %copy.8.ids_ref.refs_1_, f32[2,16,1024]{2,1,0:T(8,128)S(1)} %get-tuple-element.21.refs_3_.refs_2_, f32[2,16,1024]{2,1,0:T(8,128)S(1)} %collective-permute-done.3.refs_4_.refs_3_, ...), custom_call_target="tpu_custom_call" | custom-call | tf_op jit(solution)/shard_map/pallas_call | solution.py:206
  43.4 0.0 collective-permute-done.12.refs_4_
  43.4 0.0 collective-permute-done.13.refs_5_
  43.4 0.0 collective-permute-done.14.refs_6_
  43.4 0.0 collective-permute-done.15.refs_7_
  43.5 3.5 %collective-permute-done.16.refs_8_ = f32[2,16,1024]{2,1,0:T(8,128)S(1)} collective-permute-done((f32[2,16,1024]{2,1,0:T(8,128)S(1)}, f32[2,16,1024]{2,1,0:T(8,128)S(1)}, u32[]{:S(2)}, u32[]{:S(2)}) %collective-permute-start.16) | collective-permute-done | bytes 131104 | tf_op jit(solution)/shard_map/ppermute | solution.py:58
  46.9 1.0 %shard_map.71 = f32[2,8,16,1024]{3,2,1,0:T(8,128)} custom-call(s32[1]{0:T(128)} %bitcast.here_ref.refs_0_, f32[2,16,1024]{2,1,0:T(8,128)S(1)} %get-tuple-element.29.refs_1_, f32[2,16,1024]{2,1,0:T(8,128)S(1)} %collective-permute-done.10.refs_2_, f32[2,16,1024]{2,1,0:T(8,128)S(1)} %collective-permute-done.11.refs_3_, ...), custom_call_target="tpu_custom_call" | custom-call | tf_op jit(solution)/shard_map/pallas_call | solution.py:213
  (3 shorter events, 0.0 us)
Async XLA Ops:
  0.6 21.5 %copy-start = (f32[32,1,16,1024]{3,2,1,0:T(8,128)S(1)}, f32[32,1,16,1024]{3,2,1,0:T(8,128)}, u32[]{:S(2)}) copy-start(f32[32,1,16,1024]{3,2,1,0:T(8,128)} %param.6) | copy-start | bytes 6291460
  0.6 1.4 %copy-start.3 = (f32[1,2,128,1024]{3,2,1,0:T(8,128)S(1)}, f32[1,2,128,1024]{3,2,1,0:T(8,128)}, u32[]{:S(2)}) copy-start(f32[1,2,128,1024]{3,2,1,0:T(8,128)} %param.4) | copy-start | bytes 3145732
  2.1 6.4 %collective-permute-start.2 = (f32[8,128]{1,0:T(8,128)S(1)}, f32[8,128]{1,0:T(8,128)S(1)}, u32[]{:S(2)}, u32[]{:S(2)}) collective-permute-start(f32[8,128]{1,0:T(8,128)S(1)} %shard_map.68.refs_2_), channel_id=1, source_target_pairs={{0,3},{1,0},{2,1},{3,2},{4,7},{5,4},{6,5},{7,6},{8,11},{9,8},{10,9... | collective-permute-start | bytes 12296 | tf_op jit(solution)/shard_map/ppermute | solution.py:176
  7.2 4.5 %collective-permute-start.1 = (f32[8,128]{1,0:T(8,128)S(1)}, f32[8,128]{1,0:T(8,128)S(1)}, u32[]{:S(2)}, u32[]{:S(2)}) collective-permute-start(f32[8,128]{1,0:T(8,128)S(1)} %shard_map.68.refs_2_), channel_id=1, source_target_pairs={{0,2},{1,3},{2,0},{3,1},{4,6},{5,7},{6,4},{7,5},{8,10},{9,11},{10,... | collective-permute-start | bytes 12296 | tf_op jit(solution)/shard_map/ppermute | solution.py:176
  7.2 5.4 %collective-permute-start = (f32[8,128]{1,0:T(8,128)S(1)}, f32[8,128]{1,0:T(8,128)S(1)}, u32[]{:S(2)}, u32[]{:S(2)}) collective-permute-start(f32[8,128]{1,0:T(8,128)S(1)} %shard_map.68.refs_2_), channel_id=1, source_target_pairs={{0,1},{1,2},{2,3},{3,0},{4,5},{5,6},{6,7},{7,4},{8,9},{9,10},{10,1... | collective-permute-start | bytes 12296 | tf_op jit(solution)/shard_map/ppermute | solution.py:176
  12.6 1.2 %copy-start.4 = (f32[1,2,128,1024]{3,2,1,0:T(8,128)S(1)}, f32[1,2,128,1024]{3,2,1,0:T(8,128)}, u32[]{:S(2)}) copy-start(f32[1,2,128,1024]{3,2,1,0:T(8,128)} %param.4) | copy-start | bytes 3145732
  14.7 3.5 %collective-permute-start.3 = (f32[2,16,1024]{2,1,0:T(8,128)S(1)}, f32[2,16,1024]{2,1,0:T(8,128)S(1)}, u32[]{:S(2)}, u32[]{:S(2)}) collective-permute-start(f32[2,16,1024]{2,1,0:T(8,128)S(1)} %get-tuple-element.22), channel_id=1, source_target_pairs={{0,4},{4,0},{8,12},{12,8},{16,20},{20,16},{24,28},{28,24},{1,5},{5... | collective-permute-start | bytes 393224 | tf_op jit(solution)/shard_map/ppermute | solution.py:58
  14.7 5.9 %collective-permute-start.4 = (f32[2,16,1024]{2,1,0:T(8,128)S(1)}, f32[2,16,1024]{2,1,0:T(8,128)S(1)}, u32[]{:S(2)}, u32[]{:S(2)}) collective-permute-start(f32[2,16,1024]{2,1,0:T(8,128)S(1)} %get-tuple-element.23), channel_id=1, source_target_pairs={{0,8},{4,20},{8,0},{12,28},{16,24},{20,4},{24,16},{28,12},{1,9},{5... | collective-permute-start | bytes 393224 | tf_op jit(solution)/shard_map/ppermute | solution.py:58
  16.2 11.4 %collective-permute-start.5 = (f32[2,16,1024]{2,1,0:T(8,128)}, f32[2,16,1024]{2,1,0:T(8,128)S(1)}, u32[]{:S(2)}, u32[]{:S(2)}) collective-permute-start(f32[2,16,1024]{2,1,0:T(8,128)} %get-tuple-element.24), channel_id=1, source_target_pairs={{0,12},{4,16},{8,4},{12,24},{16,28},{20,0},{24,20},{28,8},{1,13},{... | collective-permute-start | bytes 393224 | tf_op jit(solution)/shard_map/ppermute | solution.py:58
  17.6 10.0 %collective-permute-start.6 = (f32[2,16,1024]{2,1,0:T(8,128)}, f32[2,16,1024]{2,1,0:T(8,128)S(1)}, u32[]{:S(2)}, u32[]{:S(2)}) collective-permute-start(f32[2,16,1024]{2,1,0:T(8,128)} %get-tuple-element.25), channel_id=1, source_target_pairs={{0,16},{4,12},{8,24},{12,4},{16,0},{20,28},{24,8},{28,20},{1,17},{... | collective-permute-start | bytes 393224 | tf_op jit(solution)/shard_map/ppermute | solution.py:58
  18.1 9.5 %collective-permute-start.7 = (f32[2,16,1024]{2,1,0:T(8,128)S(1)}, f32[2,16,1024]{2,1,0:T(8,128)S(1)}, u32[]{:S(2)}, u32[]{:S(2)}) collective-permute-start(f32[2,16,1024]{2,1,0:T(8,128)S(1)} %get-tuple-element.26), channel_id=1, source_target_pairs={{0,20},{4,8},{8,28},{12,0},{16,4},{20,24},{24,12},{28,16},{1,21},{... | collective-permute-start | bytes 393224 | tf_op jit(solution)/shard_map/ppermute | solution.py:58
  18.2 9.4 %collective-permute-start.8 = (f32[2,16,1024]{2,1,0:T(8,128)S(1)}, f32[2,16,1024]{2,1,0:T(8,128)S(1)}, u32[]{:S(2)}, u32[]{:S(2)}) collective-permute-start(f32[2,16,1024]{2,1,0:T(8,128)S(1)} %get-tuple-element.27), channel_id=1, source_target_pairs={{0,24},{4,28},{8,16},{12,20},{16,8},{20,12},{24,0},{28,4},{1,25},{... | collective-permute-start | bytes 393224 | tf_op jit(solution)/shard_map/ppermute | solution.py:58
  20.7 9.8 %collective-permute-start.9 = (f32[2,16,1024]{2,1,0:T(8,128)S(1)}, f32[2,16,1024]{2,1,0:T(8,128)S(1)}, u32[]{:S(2)}, u32[]{:S(2)}) collective-permute-start(f32[2,16,1024]{2,1,0:T(8,128)S(1)} %get-tuple-element.28), channel_id=1, source_target_pairs={{0,28},{4,24},{8,20},{12,16},{16,12},{20,8},{24,4},{28,0},{1,29},{... | collective-permute-start | bytes 393224 | tf_op jit(solution)/shard_map/ppermute | solution.py:58
  22.1 1.6 %copy-start.1 = (f32[32,1,16,1024]{3,2,1,0:T(8,128)S(1)}, f32[32,1,16,1024]{3,2,1,0:T(8,128)}, u32[]{:S(2)}) copy-start(f32[32,1,16,1024]{3,2,1,0:T(8,128)} %param.7) | copy-start | bytes 6291460
  27.6 10.7 %copy-start.2 = (f32[32,1,16,1024]{3,2,1,0:T(8,128)S(1)}, f32[32,1,16,1024]{3,2,1,0:T(8,128)}, u32[]{:S(2)}) copy-start(f32[32,1,16,1024]{3,2,1,0:T(8,128)} %param.7) | copy-start | bytes 6291460
  31.9 3.6 %collective-permute-start.10 = (f32[2,16,1024]{2,1,0:T(8,128)S(1)}, f32[2,16,1024]{2,1,0:T(8,128)S(1)}, u32[]{:S(2)}, u32[]{:S(2)}) collective-permute-start(f32[2,16,1024]{2,1,0:T(8,128)S(1)} %get-tuple-element.30), channel_id=1, source_target_pairs={{0,4},{4,0},{8,12},{12,8},{16,20},{20,16},{24,28},{28,24},{1,5},{5... | collective-permute-start | bytes 393224 | tf_op jit(solution)/shard_map/ppermute | solution.py:58
  32.0 5.3 %collective-permute-start.11 = (f32[2,16,1024]{2,1,0:T(8,128)S(1)}, f32[2,16,1024]{2,1,0:T(8,128)S(1)}, u32[]{:S(2)}, u32[]{:S(2)}) collective-permute-start(f32[2,16,1024]{2,1,0:T(8,128)S(1)} %get-tuple-element.31), channel_id=1, source_target_pairs={{0,8},{4,20},{8,0},{12,28},{16,24},{20,4},{24,16},{28,12},{1,9},{5... | collective-permute-start | bytes 393224 | tf_op jit(solution)/shard_map/ppermute | solution.py:58
  33.5 9.9 %collective-permute-start.12 = (f32[2,16,1024]{2,1,0:T(8,128)S(1)}, f32[2,16,1024]{2,1,0:T(8,128)S(1)}, u32[]{:S(2)}, u32[]{:S(2)}) collective-permute-start(f32[2,16,1024]{2,1,0:T(8,128)S(1)} %get-tuple-element.32), channel_id=1, source_target_pairs={{0,12},{4,16},{8,4},{12,24},{16,28},{20,0},{24,20},{28,8},{1,13},{... | collective-permute-start | bytes 393224 | tf_op jit(solution)/shard_map/ppermute | solution.py:58
  33.8 9.6 %collective-permute-start.13 = (f32[2,16,1024]{2,1,0:T(8,128)S(1)}, f32[2,16,1024]{2,1,0:T(8,128)S(1)}, u32[]{:S(2)}, u32[]{:S(2)}) collective-permute-start(f32[2,16,1024]{2,1,0:T(8,128)S(1)} %get-tuple-element.33), channel_id=1, source_target_pairs={{0,16},{4,12},{8,24},{12,4},{16,0},{20,28},{24,8},{28,20},{1,17},{... | collective-permute-start | bytes 393224 | tf_op jit(solution)/shard_map/ppermute | solution.py:58
  35.3 8.1 %collective-permute-start.14 = (f32[2,16,1024]{2,1,0:T(8,128)S(1)}, f32[2,16,1024]{2,1,0:T(8,128)S(1)}, u32[]{:S(2)}, u32[]{:S(2)}) collective-permute-start(f32[2,16,1024]{2,1,0:T(8,128)S(1)} %get-tuple-element.34), channel_id=1, source_target_pairs={{0,20},{4,8},{8,28},{12,0},{16,4},{20,24},{24,12},{28,16},{1,21},{... | collective-permute-start | bytes 393224 | tf_op jit(solution)/shard_map/ppermute | solution.py:58
  35.5 7.9 %collective-permute-start.15 = (f32[2,16,1024]{2,1,0:T(8,128)S(1)}, f32[2,16,1024]{2,1,0:T(8,128)S(1)}, u32[]{:S(2)}, u32[]{:S(2)}) collective-permute-start(f32[2,16,1024]{2,1,0:T(8,128)S(1)} %get-tuple-element.35), channel_id=1, source_target_pairs={{0,24},{4,28},{8,16},{12,20},{16,8},{20,12},{24,0},{28,4},{1,25},{... | collective-permute-start | bytes 393224 | tf_op jit(solution)/shard_map/ppermute | solution.py:58
  37.2 9.7 %collective-permute-start.16 = (f32[2,16,1024]{2,1,0:T(8,128)S(1)}, f32[2,16,1024]{2,1,0:T(8,128)S(1)}, u32[]{:S(2)}, u32[]{:S(2)}) collective-permute-start(f32[2,16,1024]{2,1,0:T(8,128)S(1)} %get-tuple-element.36), channel_id=1, source_target_pairs={{0,28},{4,24},{8,20},{12,16},{16,12},{20,8},{24,4},{28,0},{1,29},{... | collective-permute-start | bytes 393224 | tf_op jit(solution)/shard_map/ppermute | solution.py:58
